TPU v7x, 256 devices: a whole 4x4x8 slice. The times are simulated.
256 devices in a mesh: gy: 16 (over y, z_lo, core), gz: 16 (over x, z_hi).
Axes of the slice: x: 4, y: 4, z: 8 (z_hi: 4, z_lo: 2; z = z_hi * 2 + z_lo), core: 2. Of those that a mesh axis runs over, the one named last changes fastest.
Arguments:
- velocity: float32 [3, 16, 1536, 1536], P(None, None, 'gy', 'gz'), may hold values from -6 to 6
- vorticity: float32 [3, 16, 1536, 1536], P(None, None, 'gy', 'gz'), may hold values from -6 to 6
- q_state: float32 [2, 3, 16, 768, 1536], P(None, None, 'gz', 'gy'), may hold values from -6 to 6
- u_state: float32 [2, 3, 16, 768, 1536], P(None, None, 'gz', 'gy'), may hold values from -6 to 6
- shift: int32 [16], P('gz'), may hold values from 0 to 1535
- requests: int32 [16, 16, 16, 4], P('gy', 'gz'), may hold values from 0 to 191, as said below
- tracer_slot: int32 [16, 16, 16, 32], P('gy', 'gz'), may hold values from 0 to 3
- tracer_row: int32 [16, 16, 16, 32], P('gy', 'gz'), may hold values from 0 to 6
- tracer_col: int32 [16, 16, 16, 32], P('gy', 'gz'), may hold values from 0 to 94
- tracer_count: int32 [16, 16, 16], P('gy', 'gz'), may hold values from 1 to 32
- tracer_frac: float32 [2, 16, 16, 16, 32], P(None, 'gy', 'gz'), may hold values from 0 to 1
- tracer_vel: float32 [3, 16, 16, 16, 32], P(None, 'gy', 'gz'), may hold values from -6 to 6
Outputs:
- q_next: float32 [2, 3, 16, 768, 1536], P(None, None, 'gz', 'gy')
- u_next: float32 [2, 3, 16, 768, 1536], P(None, None, 'gz', 'gy')
- tracer_next: float32 [3, 16, 16, 16, 32], P(None, 'gy', 'gz')
Inputs may be any that keep to these rules, and one draw needn't show every extreme that they name: `requests`: within one owner and holder the 4 requested blocks are different blocks of that holder.
All inputs are finite; a program needn't handle non-finite values.
Results may differ from a plain program's by a relative error of at most 0.003.
Values may be sent and summed in bfloat16 or wider, within the bound.
A program may use at most 192 MiB of HBM per device.

v0:
```python
import functools
import math

import jax
import jax.numpy as jnp
import ml_dtypes
import numpy as np
from jax import lax
from jax.experimental import pallas as pl
from jax.experimental.pallas import tpu as pltpu
from jax.sharding import PartitionSpec as P

MESH = pl.DeviceIdType.MESH
BF16 = jnp.bfloat16
F32 = jnp.float32

NY = 1536
NZ = 1536
DEV = 16
LOC = 96
PLANES = 16
KZL = 48
TPP = 32
TR = DEV * TPP
MAIN = 216
PIECE = 224
QUARTER = 24
WIDE = PIECE + 80

drag_mass = 24.0
relax_ratio = 0.5
coef_keep = -5.0 / 9.0
coef_add = 15.0 / 16.0
time_step = 0.5


def dft_base(length):
    index = np.arange(length, dtype=np.int64)
    phase = (np.outer(index, index) % length).astype(np.float32) * np.float32(2.0 * math.pi / length)
    return np.cos(phase).astype(ml_dtypes.bfloat16), np.sin(phase).astype(ml_dtypes.bfloat16)


@functools.lru_cache(maxsize=None)
def tables():
    cos, sin = dft_base(NY)
    first = np.zeros((DEV, 128, DEV, 128), ml_dtypes.bfloat16)
    kz_cos = cos[:, : NZ // 2].reshape(DEV, LOC, DEV, KZL)
    kz_sin = sin[:, : NZ // 2].reshape(DEV, LOC, DEV, KZL)
    first[:, :LOC, :, :KZL] = kz_cos
    first[:, :LOC, :, KZL : 2 * KZL] = -kz_sin
    place = np.arange(NY)
    row_of = (place % 384) // QUARTER * LOC + (place // 384) * QUARTER + place % QUARTER
    second = np.concatenate([cos[row_of], sin[row_of]], axis=0)
    return first.reshape(DEV * 128, DEV * 128), second


def lane_index(shape):
    return lax.broadcasted_iota(jnp.int32, shape, len(shape) - 1)


def pack(main, last):
    lane = lane_index((QUARTER, 128))
    out = []
    for comp in range(3):
        low = last[comp * QUARTER : (comp + 1) * QUARTER]
        for third in range(3):
            at = comp * 72 + third * QUARTER
            turned = pltpu.roll(low, 96 - 32 * third, 1)
            out.append(jnp.where(lane < LOC, main[at : at + QUARTER], turned))
    out.append(jnp.zeros((8, 128), F32))
    return jnp.concatenate(out, axis=0)


def unpack_last(piece):
    lane = lane_index((QUARTER, 128))
    out = []
    for comp in range(3):
        parts = [
            pltpu.roll(piece[comp * 72 + third * QUARTER : comp * 72 + (third + 1) * QUARTER], (32 * third + 32) % 128, 1)
            for third in range(3)
        ]
        out.append(
            jnp.where(lane < 32, parts[0], jnp.where(lane < 64, parts[1], jnp.where(lane < LOC, parts[2], 0.0)))
        )
    out.append(jnp.zeros((8, 128), F32))
    return jnp.concatenate(out, axis=0)


def widen(block):
    return jnp.concatenate([block, jnp.zeros((block.shape[0], 128 - block.shape[1]), block.dtype)], axis=1)


def exchange_kernel(
    vel_hbm,
    vort_hbm,
    first_hbm,
    second_hbm,
    requests_ref,
    slot_ref,
    row_ref,
    col_ref,
    count_ref,
    frac_ref,
    tvel_ref,
    spec_hbm,
    at_ref,
    vel,
    vort,
    first,
    second,
    vel_b,
    hot,
    picked,
    spread,
    fields,
    row_lanes,
    at_cols,
    t_send,
    t_recv,
    a_send,
    a_recv,
    send1,
    recv1,
    send2,
    recv2,
    left,
    spec,
    load_sem,
    own_sem,
    out_sem,
    t_ssem,
    t_rsem,
    a_ssem,
    a_rsem,
    ssem1,
    rsem1,
    ssem2,
    rsem2,
):
    gy = lax.axis_index("gy")
    gz = lax.axis_index("gz")
    my_x, my_h = gz // 4, lax.rem(gz, 4)

    def along(base, step):
        return lax.rem(base + step, DEV)

    barrier = pltpu.get_barrier_semaphore()
    for step in range(1, DEV):
        pl.semaphore_signal(barrier, inc=1, device_id=(gy, along(gz, step)), device_id_type=MESH)
    for step in range(1, DEV):
        pl.semaphore_signal(barrier, inc=1, device_id=(along(gy, step), gz), device_id_type=MESH)
    loads = [
        pltpu.make_async_copy(vel_hbm, vel, load_sem.at[0]),
        pltpu.make_async_copy(vort_hbm, vort, load_sem.at[1]),
        pltpu.make_async_copy(first_hbm, first, load_sem.at[2]),
        pltpu.make_async_copy(second_hbm, second, load_sem.at[3]),
    ]
    for load in loads:
        load.start()

    slots = slot_ref[...]
    wanted = requests_ref[...]
    block = jnp.zeros((DEV, TPP), jnp.int32)
    for number in range(4):
        block = jnp.where(slots == number, wanted[:, number : number + 1], block)
    counts = jnp.broadcast_to(count_ref[...], (DEV, DEV))
    diagonal = lax.broadcasted_iota(jnp.int32, (DEV, DEV), 0) == lax.broadcasted_iota(jnp.int32, (DEV, DEV), 1)
    count_col = jnp.sum(jnp.where(diagonal, counts, 0).astype(F32), axis=1, keepdims=True)
    alive = (lane_index((DEV, TPP)).astype(F32) < count_col).astype(F32)
    listed = [
        (block * 8 + row_ref[...]).astype(F32),
        col_ref[...].astype(F32),
        frac_ref[0],
        frac_ref[1],
        tvel_ref[0],
        tvel_ref[1],
        tvel_ref[2],
        alive,
    ]
    t_send[...] = jnp.zeros(t_send.shape, F32)
    for peer in range(DEV):
        for number in range(8):
            t_send[peer, number : number + 1, 0:TPP] = listed[number][peer : peer + 1]

    pl.semaphore_wait(barrier, 2 * (DEV - 1))

    def to_holder(step):
        peer = along(gz, step)
        return pltpu.make_async_remote_copy(
            src_ref=t_send.at[peer],
            dst_ref=t_recv.at[gz],
            send_sem=t_ssem.at[step],
            recv_sem=t_rsem.at[step],
            device_id=(gy, peer),
            device_id_type=MESH,
        )

    for step in range(1, DEV):
        to_holder(step).start()
    own = pltpu.make_async_copy(t_send.at[gz], t_recv.at[gz], own_sem.at[0])
    own.start()

    loads[0].wait()
    for comp in range(3):
        @pl.loop(0, PLANES)
        def _(plane):
            rows = pl.ds(pl.multiple_of(plane * LOC, LOC), LOC)
            vel_b[rows, comp * 128 : (comp + 1) * 128] = widen(vel[comp, plane]).astype(BF16)

    own.wait()
    for step in range(1, DEV):
        to_holder(step).wait()

    arrived = t_recv[...]
    turned = arrived.reshape(128, 128).T
    for owner in range(DEV):
        fields[owner * TPP : (owner + 1) * TPP, :] = pltpu.roll(turned[0:TPP], (128 - owner * 8) % 128, 1)
    lane_row = lane_index((1, 128))
    for quad in range(4):
        total = jnp.zeros((1, 128), F32)
        for number in range(4):
            total = jnp.where(
                lane_row // TPP == number,
                pltpu.roll(arrived[quad * 4 + number, 0:1], number * TPP, 1),
                total,
            )
        row_lanes[0:1, quad * 128 : (quad + 1) * 128] = total

    @pl.loop(0, TR // 32)
    def _(part):
        rows = pl.ds(pl.multiple_of(part * 32, 32), 32)
        lower = pl.ds(pl.multiple_of(part * 32 + TR, 32), 32)
        start = fields[rows, 0:1]
        cell_row = lane_index((32, PLANES * LOC)).astype(F32)
        hot[rows, :] = jnp.where(cell_row == start, 1.0, 0.0).astype(BF16)
        hot[lower, :] = jnp.where(cell_row == start + 1.0, 1.0, 0.0).astype(BF16)

    @pl.loop(0, 2 * TR // 256)
    def _(part):
        rows = pl.ds(pl.multiple_of(part * 256, 256), 256)
        picked[rows, :] = jnp.dot(hot[rows, :], vel_b[...], preferred_element_type=F32)

    @pl.loop(0, TR // 32)
    def _(part):
        rows = pl.ds(pl.multiple_of(part * 32, 32), 32)
        lower = pl.ds(pl.multiple_of(part * 32 + TR, 32), 32)
        table = fields[rows, :]
        along_y, along_z = table[:, 2:3], table[:, 3:4]
        lane = lane_index((32, 128)).astype(F32)
        start = table[:, 1:2]
        cell = jnp.where(lane == start, 1.0 - along_z, jnp.where(lane == start + 1.0, along_z, 0.0))
        upper_w = (1.0 - along_y) * cell
        lower_w = along_y * cell
        ats = jnp.zeros((32, 128), F32)
        lane_i = lane_index((32, 128))
        for comp in range(3):
            cols = slice(comp * 128, (comp + 1) * 128)
            at = jnp.sum(upper_w * picked[rows, cols] + lower_w * picked[lower, cols], axis=1, keepdims=True)
            ats = jnp.where(lane_i == comp, at, ats)
            drag = drag_mass * table[:, 7:8] * (table[:, 4 + comp : 5 + comp] - at)
            for weight, place in ((upper_w, rows), (lower_w, lower)):
                value = weight * drag
                high = value.astype(BF16)
                spread[place, comp * 256 : comp * 256 + 128] = high
                spread[place, comp * 256 + 128 : (comp + 1) * 256] = (value - high.astype(F32)).astype(BF16)
        at_cols[rows, :] = ats

    loads[1].wait()
    order = [(dx, dh) for dh in (2, 1, 3, 0) for dx in (2, 1, 3, 0)]

    def target(dx, dh):
        return lax.rem(my_x + dx, 4) * 4 + lax.rem(my_h + dh, 4)

    def of_step(step):
        quarter, third = step // 4, lax.rem(step, 4)
        far = lambda n: jnp.where(n == 0, 2, jnp.where(n == 1, 1, jnp.where(n == 2, 3, 0)))
        return far(third), far(quarter)

    def to_plane(step):
        dx, dh = of_step(step)
        peer = target(dx, dh)
        return pltpu.make_async_remote_copy(
            src_ref=send1.at[peer],
            dst_ref=recv1.at[pl.ds(0, PIECE), pl.ds(pl.multiple_of(gz * 128, 128), 128)],
            send_sem=ssem1.at[step],
            recv_sem=rsem1.at[step],
            device_id=(gy, peer),
            device_id_type=MESH,
        )

    def make_plane(plane):
        base = plane * LOC
        cell_row = (lax.broadcasted_iota(jnp.int32, (LOC, TR), 0) + base).astype(F32)
        starts = row_lanes[0:1, :]
        upper = jnp.where(cell_row == starts, 1.0, 0.0).astype(BF16)
        lower = jnp.where(cell_row == starts + 1.0, 1.0, 0.0).astype(BF16)
        both = jnp.concatenate([upper, lower], axis=1)
        u = [widen(vel[comp, plane]) for comp in range(3)]
        w = [widen(vort[comp, plane]) for comp in range(3)]
        mains, lasts = [], []
        for comp in range(3):
            a, b = (comp + 1) % 3, (comp + 2) % 3
            fed = jnp.dot(both, spread[:, comp * 256 : (comp + 1) * 256], preferred_element_type=F32)
            force = (u[a] * w[b] - u[b] * w[a]) + (fed[:, 0:128] + fed[:, 128:256])
            mains.append(force[0:72])
            lasts.append(force[72:96])
        send1[plane] = pack(jnp.concatenate(mains, axis=0), jnp.concatenate(lasts, axis=0)).astype(BF16)

    @pl.loop(0, DEV - 1)
    def _(step):
        dx, dh = of_step(step)
        make_plane(target(dx, dh))
        to_plane(step).start()

    make_plane(gz)
    own1 = pltpu.make_async_copy(
        send1.at[gz], recv1.at[pl.ds(0, PIECE), pl.ds(pl.multiple_of(gz * 128, 128), 128)], own_sem.at[1]
    )
    own1.start()

    total = jnp.zeros((TPP, 128), F32)
    lane_i = lane_index((TPP, 128))
    for owner in range(DEV):
        moved = pltpu.roll(at_cols[owner * TPP : (owner + 1) * TPP, :], owner * 8, 1)
        total = jnp.where(lane_i // 8 == owner, moved, total)
    back = jnp.concatenate([total, jnp.zeros((128 - TPP, 128), F32)], axis=0).T
    a_send[...] = back.reshape(DEV, 8, 128)

    def to_owner(step):
        peer = along(gz, step)
        return pltpu.make_async_remote_copy(
            src_ref=a_send.at[peer],
            dst_ref=a_recv.at[gz],
            send_sem=a_ssem.at[step],
            recv_sem=a_rsem.at[step],
            device_id=(gy, peer),
            device_id_type=MESH,
        )

    for step in range(1, DEV):
        to_owner(step).start()
    own2 = pltpu.make_async_copy(a_send.at[gz], a_recv.at[gz], own_sem.at[2])
    own2.start()

    own1.wait()

    @pl.loop(0, DEV - 1)
    def _(step):
        to_plane(step).wait()

    @pl.loop(0, DEV)
    def _(source):
        cols = pl.ds(pl.multiple_of(source * 128, 128), 128)
        piece = recv1[0:PIECE, cols].astype(F32)
        recv1[PIECE:WIDE, cols] = unpack_last(piece).astype(BF16)

    loads[2].wait()

    def to_owner_kz(step):
        peer = lax.rem(gy // 2 + step // 2, 8) * 2 + lax.rem(gy + step, 2)
        return pltpu.make_async_remote_copy(
            src_ref=send2.at[peer],
            dst_ref=recv2.at[gy],
            send_sem=ssem2.at[step],
            recv_sem=rsem2.at[step],
            device_id=(peer, gz),
            device_id_type=MESH,
        )

    def make_pair(turn):
        pair = lax.rem(gy // 2 + turn, 8)
        cols = pl.ds(pl.multiple_of(pair * 256, 256), 256)
        out = jnp.dot(recv1[...], first[:, cols], preferred_element_type=F32)
        for half in range(2):
            lanes = slice(half * 128, (half + 1) * 128)
            send2[pair * 2 + half] = pack(out[0:MAIN, lanes], out[PIECE : PIECE + 72, lanes]).astype(BF16)

    @pl.loop(1, 8)
    def _(turn):
        make_pair(turn)
        to_owner_kz(2 * turn).start()
        to_owner_kz(2 * turn + 1).start()

    make_pair(0)
    to_owner_kz(1).start()
    own3 = pltpu.make_async_copy(send2.at[gy], recv2.at[gy], own_sem.at[3])
    own3.start()

    own2.wait()
    for step in range(1, DEV):
        to_owner(step).wait()
    at_ref[...] = a_recv[...]

    own3.wait()

    @pl.loop(1, DEV)
    def _(step):
        to_owner_kz(step).wait()

    for comp in range(3):
        for third in range(3):
            at = comp * 72 + third * QUARTER
            stacked = recv2[:, 0:PIECE, :].astype(F32)[:, at : at + QUARTER].reshape(DEV * QUARTER, 128)
            for part in range(3):
                tile = stacked[part * 128 : (part + 1) * 128].T
                cols = slice(third * 384 + part * 128, third * 384 + (part + 1) * 128)
                real, imag = tile[0:KZL].astype(BF16), tile[KZL : 2 * KZL].astype(BF16)
                rows_re = slice(comp * KZL, (comp + 1) * KZL)
                rows_im = slice((3 + comp) * KZL, (4 + comp) * KZL)
                more = slice(NY + cols.start, NY + cols.stop)
                left[rows_re, cols] = real
                left[rows_re, more] = imag
                left[rows_im, cols] = imag
                left[rows_im, more] = -real
                last_cols = slice(1152 + part * 128, 1152 + (part + 1) * 128)
                last_more = slice(NY + last_cols.start, NY + last_cols.stop)
                for piece in range(2):
                    lo = third * 32 + piece * 16
                    value = tile[96 + piece * 16 : 112 + piece * 16].astype(BF16)
                    if lo < KZL:
                        left[comp * KZL + lo : comp * KZL + lo + 16, last_cols] = value
                        left[(3 + comp) * KZL + lo : (3 + comp) * KZL + lo + 16, last_more] = -value
                    else:
                        lo -= KZL
                        left[comp * KZL + lo : comp * KZL + lo + 16, last_more] = value
                        left[(3 + comp) * KZL + lo : (3 + comp) * KZL + lo + 16, last_cols] = value

    loads[3].wait()

    def write(tile):
        cols = pl.ds(pl.multiple_of(tile * 256, 256), 256)
        return pltpu.make_async_copy(spec.at[:, cols], spec_hbm.at[:, cols], out_sem.at[tile])

    @pl.loop(0, NY // 256)
    def _(tile):
        cols = pl.ds(pl.multiple_of(tile * 256, 256), 256)
        spec[:, cols] = jnp.dot(left[...], second[:, cols], preferred_element_type=F32)
        write(tile).start()

    @pl.loop(0, NY // 256)
    def _(tile):
        write(tile).wait()


def update_kernel(shift_ref, spec_ref, q_ref, u_ref, at_ref, count_ref, tvel_ref, q_out, u_out, t_out):
    rows = q_ref.shape[2]
    kz_first = lax.axis_index("gy") * KZL + pl.program_id(0) * rows
    shift = shift_ref[0]
    ky = lane_index((rows, NY))
    kys = jnp.where(ky < NY // 2, ky, ky - NY).astype(F32)
    kz = (lax.broadcasted_iota(jnp.int32, (rows, NY), 0) + kz_first).astype(F32)
    wave_square = kz * kz + kys * kys
    inverse = 1.0 / jnp.maximum(wave_square, 1.0)
    scale = 1.0 / math.sqrt(NY * NZ)
    damping = (time_step * scale) * jnp.exp(-2.0 * wave_square / (NY * NZ))
    for part in range(2):
        moved = [pltpu.roll(spec_ref[part, comp], shift, 1) for comp in range(3)]
        radial = (kys * moved[1] + kz * moved[2]) * inverse
        projected = [moved[0], moved[1] - kys * radial, moved[2] - kz * radial]
        for comp in range(3):
            q_new = coef_keep * q_ref[part, comp] + damping * projected[comp]
            q_out[part, comp] = q_new
            u_out[part, comp] = u_ref[part, comp] + coef_add * q_new

    counts = jnp.broadcast_to(count_ref[...], (DEV, DEV))
    diagonal = lax.broadcasted_iota(jnp.int32, (DEV, DEV), 0) == lax.broadcasted_iota(jnp.int32, (DEV, DEV), 1)
    count_col = jnp.sum(jnp.where(diagonal, counts, 0).astype(F32), axis=1, keepdims=True)
    alive = (lane_index((DEV, TPP)).astype(F32) < count_col).astype(F32)
    for comp in range(3):
        old = tvel_ref[comp]
        at = jnp.concatenate([at_ref[peer, comp : comp + 1, 0:TPP] for peer in range(DEV)], axis=0)
        t_out[comp] = old + relax_ratio * alive * (at - old)


def on_device(
    velocity,
    vorticity,
    q_state,
    u_state,
    shift,
    requests,
    tracer_slot,
    tracer_row,
    tracer_col,
    tracer_count,
    tracer_frac,
    tracer_vel,
):
    first, second = tables()
    hbm = pl.BlockSpec(memory_space=pl.ANY)
    vmem = pl.BlockSpec(memory_space=pltpu.VMEM)
    count = tracer_count.reshape(1, DEV)
    old = tracer_vel.reshape(3, DEV, TPP)
    spectrum, at_tracer = pl.pallas_call(
        exchange_kernel,
        out_shape=(
            jax.ShapeDtypeStruct((6 * KZL, NY), F32),
            jax.ShapeDtypeStruct((DEV, 8, 128), F32),
        ),
        in_specs=[hbm] * 4 + [vmem] * 7,
        out_specs=(hbm, vmem),
        scratch_shapes=[
            pltpu.VMEM((3, PLANES, LOC, LOC), F32),
            pltpu.VMEM((3, PLANES, LOC, LOC), F32),
            pltpu.VMEM((DEV * 128, DEV * 128), BF16),
            pltpu.VMEM((2 * NY, NY), BF16),
            pltpu.VMEM((PLANES * LOC, 384), BF16),
            pltpu.VMEM((2 * TR, PLANES * LOC), BF16),
            pltpu.VMEM((2 * TR, 384), F32),
            pltpu.VMEM((2 * TR, 768), BF16),
            pltpu.VMEM((TR, 128), F32),
            pltpu.VMEM((8, TR), F32),
            pltpu.VMEM((TR, 128), F32),
            pltpu.VMEM((DEV, 8, 128), F32),
            pltpu.VMEM((DEV, 8, 128), F32),
            pltpu.VMEM((DEV, 8, 128), F32),
            pltpu.VMEM((DEV, 8, 128), F32),
            pltpu.VMEM((DEV, PIECE, 128), BF16),
            pltpu.VMEM((WIDE, DEV * 128), BF16),
            pltpu.VMEM((DEV, PIECE, 128), BF16),
            pltpu.VMEM((DEV, PIECE, 128), BF16),
            pltpu.VMEM((6 * KZL, 2 * NY), BF16),
            pltpu.VMEM((6 * KZL, NY), F32),
            pltpu.SemaphoreType.DMA((4,)),
            pltpu.SemaphoreType.DMA((4,)),
            pltpu.SemaphoreType.DMA((NY // 256,)),
        ]
        + [pltpu.SemaphoreType.DMA((DEV,))] * 8,
        compiler_params=pltpu.CompilerParams(
            collective_id=0, has_side_effects=True, vmem_limit_bytes=56 * 2**20
        ),
        cost_estimate=pl.CostEstimate(flops=6 * 10**9, bytes_accessed=25 * 2**20, transcendentals=0),
        name="exchange",
    )(
        velocity,
        vorticity,
        jnp.asarray(first),
        jnp.asarray(second),
        requests.reshape(DEV, 4),
        tracer_slot.reshape(DEV, TPP),
        tracer_row.reshape(DEV, TPP),
        tracer_col.reshape(DEV, TPP),
        count,
        tracer_frac.reshape(2, DEV, TPP),
        old,
    )
    rows = 8
    part = pl.BlockSpec((2, 3, rows, NY), lambda i: (0, 0, i, 0))

    def whole(*shape):
        return pl.BlockSpec(shape, lambda i: (0,) * len(shape))

    q_next, u_next, tracer_next = pl.pallas_call(
        update_kernel,
        grid=(KZL // rows,),
        out_shape=(
            jax.ShapeDtypeStruct((2, 3, KZL, NY), F32),
            jax.ShapeDtypeStruct((2, 3, KZL, NY), F32),
            jax.ShapeDtypeStruct((3, DEV, TPP), F32),
        ),
        in_specs=[
            pl.BlockSpec(memory_space=pltpu.SMEM),
            part,
            part,
            part,
            whole(DEV, 8, 128),
            whole(1, DEV),
            whole(3, DEV, TPP),
        ],
        out_specs=(part, part, whole(3, DEV, TPP)),
        compiler_params=pltpu.CompilerParams(vmem_limit_bytes=32 * 2**20),
        name="update",
    )(
        shift,
        spectrum.reshape(2, 3, KZL, NY),
        q_state.reshape(2, 3, KZL, NY),
        u_state.reshape(2, 3, KZL, NY),
        at_tracer,
        count,
        old,
    )
    return (
        q_next.reshape(q_state.shape),
        u_next.reshape(u_state.shape),
        tracer_next.reshape(tracer_vel.shape),
    )


def solution(mesh):
    return jax.shard_map(
        on_device,
        mesh=mesh,
        in_specs=(
            P(None, None, "gy", "gz"),
            P(None, None, "gy", "gz"),
            P(None, None, "gz", "gy", None),
            P(None, None, "gz", "gy", None),
            P("gz"),
            P("gy", "gz", None, None),
            P("gy", "gz", None, None),
            P("gy", "gz", None, None),
            P("gy", "gz", None, None),
            P("gy", "gz", None),
            P(None, "gy", "gz", None, None),
            P(None, "gy", "gz", None, None),
        ),
        out_specs=(
            P(None, None, "gz", "gy", None),
            P(None, None, "gz", "gy", None),
            P(None, "gy", "gz", None, None),
        ),
        check_vma=False,
    )
```

profile of v0, /device:TPU:1, one launch (start us, length us, event | category | flops | bytes accessed | tf_op | source)
XLA Modules:
  0.0 81.0 jit_solution(6841007561362409618)
XLA Ops:
  1.3 1.4 %copy.17.requests_ref = s32[16,4]{1,0:T(8,128)} copy(s32[16,4]{0,1:T(4,128)} %bitcast.30) | data formatting | bytes 512 | tf_op jit(solution)/shard_map/reshape | solution.py:539
  2.6 0.0 copy-start
  2.6 0.0 copy-start.1
  2.6 0.0 copy-start.3
  2.6 0.0 copy-start.5
  2.6 72.4 %exchange.1 = (f32[288,1536]{1,0:T(8,128)}, f32[16,8,128]{2,1,0:T(8,128)}) custom-call(f32[3,16,96,96]{3,2,1,0:T(8,128)} %vel_hbm.1, f32[3,16,96,96]{3,2,1,0:T(8,128)} %vort_hbm.1, bf16[2048,2048]{1,0:T(8,128)(2,1)} %constant.4.clone.first_hbm, bf16[3072,1536]{1,0:T(8,128)(2,1)} %constant.5.clone.second_hbm, s32[16,4]{1,0:T(8,128)} %copy.17.requests_ref, ...), custom_call_target="tpu_custom_call" | custom-call | flops 6000000000 | bytes 26214400 | tf_op jit(solution)/shard_map/exchange/pallas_call | solution.py:494
  75.0 0.0 copy-done
  75.0 0.0 copy-done.1
  75.0 0.0 copy-done.3
  75.0 0.0 copy-done.5
  75.0 0.0 copy-start.2
  75.1 1.5 %copy-done.2 = f32[288,1536]{1,0:T(8,128)S(1)} copy-done((f32[288,1536]{1,0:T(8,128)S(1)}, f32[288,1536]{1,0:T(8,128)}, u32[]{:S(2)}) %copy-start.2) | copy-done | bytes 1769496
  76.5 0.0 copy-start.4
  76.5 0.8 %copy-done.4 = f32[16,8,128]{2,1,0:T(8,128)S(1)} copy-done((f32[16,8,128]{2,1,0:T(8,128)S(1)}, f32[16,8,128]{2,1,0:T(8,128)}, u32[]{:S(2)}) %copy-start.4) | copy-done | bytes 65560
  77.4 3.7 %update.1 = (f32[2,3,48,1536]{3,2,1,0:T(8,128)}, f32[2,3,48,1536]{3,2,1,0:T(8,128)}, f32[3,16,32]{2,1,0:T(8,128)}) custom-call(s32[1]{0:T(128)S(6)} %copy.21.shift_ref, f32[2,3,48,1536]{3,2,1,0:T(8,128)S(1)} %bitcast.21, f32[2,3,48,1536]{3,2,1,0:T(8,128)S(1)} %bitcast.19, f32[2,3,48,1536]{3,2,1,0:T(8,128)S(1)} %bitcast.20, f32[16,8,128]{2,1,0:T(8,128)S(1)} %copy-done.4, ...), custom_call_target="tpu_custom_call" | custom-call | tf_op jit(solution)/shard_map/update/pallas_call | solution.py:553
Async XLA Ops:
  2.6 72.4 %copy-start = (f32[2,3,1,48,1536]{4,3,2,1,0:T(8,128)S(1)}, f32[2,3,1,48,1536]{4,3,2,1,0:T(8,128)}, u32[]{:S(2)}) copy-start(f32[2,3,1,48,1536]{4,3,2,1,0:T(8,128)} %param.16) | copy-start | bytes 5308420
  2.6 72.4 %copy-start.1 = (f32[2,3,1,48,1536]{4,3,2,1,0:T(8,128)S(1)}, f32[2,3,1,48,1536]{4,3,2,1,0:T(8,128)}, u32[]{:S(2)}) copy-start(f32[2,3,1,48,1536]{4,3,2,1,0:T(8,128)} %param.17) | copy-start | bytes 5308420
  2.6 72.4 %copy-start.3 = (f32[3,1,1,16,32]{4,3,2,1,0:T(8,128)S(1)}, f32[3,1,1,16,32]{4,3,2,1,0:T(8,128)}, u32[]{:S(2)}) copy-start(f32[3,1,1,16,32]{4,3,2,1,0:T(8,128)} %param.25) | copy-start | bytes 18436
  2.6 72.4 %copy-start.5 = (s32[1,1,16]{2,1,0:T(1,128)S(1)}, s32[1,1,16]{2,1,0:T(1,128)}, u32[]{:S(2)}) copy-start(s32[1,1,16]{2,1,0:T(1,128)} %param.23) | copy-start | bytes 196
  75.0 1.5 %copy-start.2 = (f32[288,1536]{1,0:T(8,128)S(1)}, f32[288,1536]{1,0:T(8,128)}, u32[]{:S(2)}) copy-start(f32[288,1536]{1,0:T(8,128)} %get-tuple-element.8) | copy-start | bytes 5308420
  76.5 0.8 %copy-start.4 = (f32[16,8,128]{2,1,0:T(8,128)S(1)}, f32[16,8,128]{2,1,0:T(8,128)}, u32[]{:S(2)}) copy-start(f32[16,8,128]{2,1,0:T(8,128)} %get-tuple-element.9.at_ref) | copy-start | bytes 196612
where the time goes:
time: 81.3 us; the launch traced here: 81 us
  Pallas kernels  76 us (93%)
  local copies, waits for them, and re-layouts  3.68 us (5%)
  between operations  1.33 us (2%)
    pallas_call x1, Pallas kernels, on_device(): pl.pallas_call(exchange_kernel, out_shape=(jax.ShapeDtypeStruct((6 * KZL,...  72.4 us
    pallas_call x1, Pallas kernels, on_device(): pl.pallas_call(update_kernel, grid=(KZL // rows,), out_shape=(jax.ShapeDt...  3.68 us
    unnamed x12, local copies, waits for them, and re-layouts  2.32 us

commit v1 on v0

v1 whole, which is shorter than its diff:
```python
import functools
import math

import jax
import jax.numpy as jnp
import ml_dtypes
import numpy as np
from jax import lax
from jax.experimental import pallas as pl
from jax.experimental.pallas import tpu as pltpu
from jax.sharding import PartitionSpec as P

MESH = pl.DeviceIdType.MESH
BF16 = jnp.bfloat16
F32 = jnp.float32

NY = 1536
NZ = 1536
DEV = 16
LOC = 96
PLANES = 16
CELL_ROWS = PLANES * LOC
BLOCKS = 192
KZL = 48
TPP = 32
TR = DEV * TPP
QUARTER = 24
SPLIT = ((0, 16), (16, 8))
MAIN = (144, 72)
PIECE = (144, 80)
LAST = (48, 24)
WIDE = (192, 112)
DEPTH = (2048, 1024)

drag_mass = 24.0
relax_ratio = 0.5
coef_keep = -5.0 / 9.0
coef_add = 15.0 / 16.0
time_step = 0.5


def dft_base(length):
    index = np.arange(length, dtype=np.int64)
    phase = (np.outer(index, index) % length).astype(np.float32) * np.float32(2.0 * math.pi / length)
    return np.cos(phase).astype(ml_dtypes.bfloat16), np.sin(phase).astype(ml_dtypes.bfloat16)


@functools.lru_cache(maxsize=None)
def tables():
    cos, sin = dft_base(NY)
    first = np.zeros((DEV, 128, DEV, 128), ml_dtypes.bfloat16)
    kz_cos = cos[:, : NZ // 2].reshape(DEV, LOC, DEV, KZL)
    kz_sin = sin[:, : NZ // 2].reshape(DEV, LOC, DEV, KZL)
    first[:, :LOC, :, :KZL] = kz_cos
    first[:, :LOC, :, KZL : 2 * KZL] = -kz_sin
    second = []
    for low, rows in SPLIT:
        quarter = np.arange(4)[:, None, None]
        source = np.arange(DEV)[None, :, None]
        row = np.arange(rows)[None, None, :]
        row_of = (source * LOC + quarter * QUARTER + low + row).reshape(-1)
        second += [cos[row_of], sin[row_of]]
    return first.reshape(DEV * 128, DEV * 128), np.concatenate(second, axis=0)


def lane_index(shape):
    return lax.broadcasted_iota(jnp.int32, shape, len(shape) - 1)


def pack(main, last, part):
    rows = SPLIT[part][1]
    lane = lane_index((rows, 128))
    out = []
    for comp in range(3):
        low = last[comp * rows : (comp + 1) * rows]
        for third in range(3):
            at = (comp * 3 + third) * rows
            turned = pltpu.roll(low, 96 - 32 * third, 1)
            out.append(jnp.where(lane < LOC, main[at : at + rows], turned))
    if PIECE[part] > MAIN[part]:
        out.append(jnp.zeros((PIECE[part] - MAIN[part], 128), F32))
    return jnp.concatenate(out, axis=0)


def unpack_last(piece, part):
    rows = SPLIT[part][1]
    lane = lane_index((rows, 128))
    out = []
    for comp in range(3):
        parts = [
            pltpu.roll(
                piece[(comp * 3 + third) * rows : (comp * 3 + third + 1) * rows], (32 * third + 32) % 128, 1
            )
            for third in range(3)
        ]
        out.append(
            jnp.where(lane < 32, parts[0], jnp.where(lane < 64, parts[1], jnp.where(lane < LOC, parts[2], 0.0)))
        )
    rest = WIDE[part] - PIECE[part] - LAST[part]
    if rest:
        out.append(jnp.zeros((rest, 128), F32))
    return jnp.concatenate(out, axis=0)


def widen(block):
    return jnp.concatenate([block, jnp.zeros((block.shape[0], 128 - block.shape[1]), block.dtype)], axis=1)


def exchange_kernel(
    vel_hbm,
    vort_hbm,
    first_hbm,
    second_hbm,
    requests_ref,
    slot_ref,
    row_ref,
    col_ref,
    count_ref,
    frac_ref,
    tvel_ref,
    spec_hbm,
    at_ref,
    vel,
    vort,
    cross,
    first,
    second,
    vel_b,
    hot,
    picked,
    spread,
    row_lanes,
    t_send,
    t_recv,
    a_send,
    a_recv,
    send1a,
    send1b,
    recv1a,
    recv1b,
    send2a,
    send2b,
    recv2a,
    recv2b,
    left_a,
    left_b,
    spec,
    load_sem,
    own_sem,
    out_sem,
    t_ssem,
    t_rsem,
    a_ssem,
    a_rsem,
    ssem1a,
    rsem1a,
    ssem1b,
    rsem1b,
    ssem2a,
    rsem2a,
    ssem2b,
    rsem2b,
):
    gy = lax.axis_index("gy")
    gz = lax.axis_index("gz")
    my_x, my_h = gz // 4, lax.rem(gz, 4)
    send1, recv1 = (send1a, send1b), (recv1a, recv1b)
    send2, recv2 = (send2a, send2b), (recv2a, recv2b)
    sems1 = ((ssem1a, rsem1a), (ssem1b, rsem1b))
    sems2 = ((ssem2a, rsem2a), (ssem2b, rsem2b))
    left = (left_a, left_b)

    def along(base, step):
        return lax.rem(base + step, DEV)

    barrier = pltpu.get_barrier_semaphore()
    for step in range(1, DEV):
        pl.semaphore_signal(barrier, inc=1, device_id=(gy, along(gz, step)), device_id_type=MESH)
    for step in range(1, DEV):
        pl.semaphore_signal(barrier, inc=1, device_id=(along(gy, step), gz), device_id_type=MESH)
    loads = [
        pltpu.make_async_copy(vel_hbm, vel, load_sem.at[0]),
        pltpu.make_async_copy(vort_hbm, vort, load_sem.at[1]),
        pltpu.make_async_copy(first_hbm, first, load_sem.at[2]),
        pltpu.make_async_copy(second_hbm, second, load_sem.at[3]),
    ]
    for load in loads:
        load.start()

    slots = slot_ref[...]
    wanted = requests_ref[...]
    block = jnp.zeros((DEV, TPP), jnp.int32)
    for number in range(4):
        block = jnp.where(slots == number, wanted[:, number : number + 1], block)
    counts = jnp.broadcast_to(count_ref[...], (DEV, DEV))
    diagonal = lax.broadcasted_iota(jnp.int32, (DEV, DEV), 0) == lax.broadcasted_iota(jnp.int32, (DEV, DEV), 1)
    count_col = jnp.sum(jnp.where(diagonal, counts, 0).astype(F32), axis=1, keepdims=True)
    alive = (lane_index((DEV, TPP)).astype(F32) < count_col).astype(F32)
    upper = [(block * 8 + row_ref[...]).astype(F32), col_ref[...].astype(F32), frac_ref[0], frac_ref[1]]
    lower = [tvel_ref[0], tvel_ref[1], tvel_ref[2], alive]
    t_send[:, 0, :] = jnp.concatenate(upper, axis=1)
    t_send[:, 1, :] = jnp.concatenate(lower, axis=1)

    pl.semaphore_wait(barrier, 2 * (DEV - 1))

    def to_holder(step):
        peer = along(gz, step)
        return pltpu.make_async_remote_copy(
            src_ref=t_send.at[peer],
            dst_ref=t_recv.at[gz],
            send_sem=t_ssem.at[step],
            recv_sem=t_rsem.at[step],
            device_id=(gy, peer),
            device_id_type=MESH,
        )

    for step in range(1, DEV):
        to_holder(step).start()
    own = pltpu.make_async_copy(t_send.at[gz], t_recv.at[gz], own_sem.at[0])
    own.start()

    loads[0].wait()
    for comp in range(3):
        for row in range(8):
            cols = slice(comp * 1024 + row * 128, comp * 1024 + (row + 1) * 128)
            vel_b[0:BLOCKS, cols] = widen(vel[comp, pl.ds(row, BLOCKS, stride=8), :]).astype(BF16)
    vel_b[BLOCKS:256, :] = jnp.zeros((256 - BLOCKS, 3072), BF16)
    loads[1].wait()

    @pl.loop(0, PLANES)
    def _(plane):
        rows = pl.ds(pl.multiple_of(plane * LOC, LOC), LOC)
        u = [vel[comp, rows, :] for comp in range(3)]
        w = [vort[comp, rows, :] for comp in range(3)]
        for comp in range(3):
            a, b = (comp + 1) % 3, (comp + 2) % 3
            cross[plane, comp * LOC : (comp + 1) * LOC, :] = widen(u[a] * w[b] - u[b] * w[a])

    own.wait()
    for step in range(1, DEV):
        to_holder(step).wait()

    upper = t_recv[:, 0, :]
    lower = t_recv[:, 1, :]
    turned = jnp.concatenate([upper, lower, jnp.zeros((128 - 2 * DEV, 128), F32)], axis=0).T
    lane_row = lane_index((1, 128))
    for quad in range(4):
        total = jnp.zeros((1, 128), F32)
        for number in range(4):
            owner = quad * 4 + number
            total = jnp.where(
                lane_row // TPP == number, pltpu.roll(upper[owner : owner + 1], number * TPP, 1), total
            )
        row_lanes[0:1, quad * 128 : (quad + 1) * 128] = total

    def field(number, owner):
        rows = slice((number % 4) * TPP, (number % 4 + 1) * TPP)
        col = (number // 4) * DEV + owner
        return jnp.broadcast_to(turned[rows, col : col + 1], (TPP, 128))

    lane = lane_index((TPP, 128))
    lane_f = lane.astype(F32)
    for owner in range(DEV):
        block_at = (field(0, owner).astype(jnp.int32) // 8)
        rows = slice(owner * TPP, (owner + 1) * TPP)
        hot[rows, 0:128] = jnp.where(lane == block_at, 1.0, 0.0).astype(BF16)
        hot[rows, 128:256] = jnp.where(lane + 128 == block_at, 1.0, 0.0).astype(BF16)

    @pl.loop(0, 6)
    def _(tile):
        cols = pl.ds(pl.multiple_of(tile * 512, 512), 512)
        picked[:, cols] = jnp.dot(hot[...], vel_b[:, cols], preferred_element_type=F32)

    back = jnp.zeros((TPP, 128), F32)
    for owner in range(DEV):
        rows = slice(owner * TPP, (owner + 1) * TPP)
        lows = slice(TR + owner * TPP, TR + (owner + 1) * TPP)
        row = jnp.bitwise_and(field(0, owner).astype(jnp.int32), 7)
        start, along_y, along_z = field(1, owner), field(2, owner), field(3, owner)
        cell = jnp.where(lane_f == start, 1.0 - along_z, jnp.where(lane_f == start + 1.0, along_z, 0.0))
        upper_w = (1.0 - along_y) * cell
        lower_w = along_y * cell
        picks = [
            jnp.where(row == number, 1.0 - along_y, jnp.where(row + 1 == number, along_y, 0.0))
            for number in range(8)
        ]
        mass = drag_mass * field(7, owner)
        for comp in range(3):
            line = picks[0] * picked[rows, comp * 1024 : comp * 1024 + 128]
            for number in range(1, 8):
                line += picks[number] * picked[rows, comp * 1024 + number * 128 : comp * 1024 + (number + 1) * 128]
            at = jnp.sum(cell * line, axis=1, keepdims=True)
            back = jnp.where(lane == comp * DEV + owner, at, back)
            drag = mass * (field(4 + comp, owner) - at)
            for weight, place in ((upper_w, rows), (lower_w, lows)):
                value = weight * drag
                high = value.astype(BF16)
                spread[place, comp * 256 : comp * 256 + 128] = high
                spread[place, comp * 256 + 128 : (comp + 1) * 256] = (value - high.astype(F32)).astype(BF16)

    def far(number):
        return jnp.where(number == 0, 2, jnp.where(number == 1, 1, jnp.where(number == 2, 3, 0)))

    def plane_of(step):
        dx, dh = far(lax.rem(step, 4)), far(step // 4)
        return lax.rem(my_x + dx, 4) * 4 + lax.rem(my_h + dh, 4)

    def landing(part):
        return recv1[part].at[pl.ds(0, PIECE[part]), pl.ds(pl.multiple_of(gz * 128, 128), 128)]

    def to_plane(step, part):
        peer = plane_of(step)
        return pltpu.make_async_remote_copy(
            src_ref=send1[part].at[peer],
            dst_ref=landing(part),
            send_sem=sems1[part][0].at[step],
            recv_sem=sems1[part][1].at[step],
            device_id=(gy, peer),
            device_id_type=MESH,
        )

    def own_plane(part):
        return pltpu.make_async_copy(send1[part].at[gz], landing(part), own_sem.at[1 + part])

    starts = row_lanes[0:1, :]

    @pl.loop(0, DEV // 2)
    def _(turn):
        planes = [plane_of(2 * turn), plane_of(2 * turn + 1)]
        hots = []
        for plane in planes:
            cell_row = (lax.broadcasted_iota(jnp.int32, (LOC, TR), 0) + plane * LOC).astype(F32)
            up = jnp.where(cell_row == starts, 1.0, 0.0).astype(BF16)
            down = jnp.where(cell_row == starts + 1.0, 1.0, 0.0).astype(BF16)
            hots.append(jnp.concatenate([up, down], axis=1))
        both = jnp.concatenate(hots, axis=0)
        forces = [[], []]
        for comp in range(3):
            fed = jnp.dot(both, spread[:, comp * 256 : (comp + 1) * 256], preferred_element_type=F32)
            for half in range(2):
                mine = fed[half * LOC : (half + 1) * LOC]
                forces[half].append(
                    cross[planes[half], comp * LOC : (comp + 1) * LOC, :] + (mine[:, 0:128] + mine[:, 128:256])
                )
        for half in range(2):
            for part in range(2):
                low, rows = SPLIT[part]
                main = [
                    forces[half][comp][third * QUARTER + low : third * QUARTER + low + rows]
                    for comp in range(3)
                    for third in range(3)
                ]
                last = [forces[half][comp][72 + low : 72 + low + rows] for comp in range(3)]
                send1[part][planes[half]] = pack(
                    jnp.concatenate(main, axis=0), jnp.concatenate(last, axis=0), part
                ).astype(BF16)
        to_plane(2 * turn, 0).start()

        @pl.when(turn < DEV // 2 - 1)
        def _():
            to_plane(2 * turn + 1, 0).start()

    own_plane(0).start()

    @pl.loop(0, DEV - 1)
    def _(step):
        to_plane(step, 1).start()

    own_plane(1).start()

    done = jnp.concatenate([back, jnp.zeros((128 - TPP, 128), F32)], axis=0).T
    a_send[:, 0, :] = (
        done[0:DEV] + pltpu.roll(done[DEV : 2 * DEV], TPP, 1) + pltpu.roll(done[2 * DEV : 3 * DEV], 2 * TPP, 1)
    )

    def to_owner(step):
        peer = along(gz, step)
        return pltpu.make_async_remote_copy(
            src_ref=a_send.at[peer],
            dst_ref=a_recv.at[gz],
            send_sem=a_ssem.at[step],
            recv_sem=a_rsem.at[step],
            device_id=(gy, peer),
            device_id_type=MESH,
        )

    for step in range(1, DEV):
        to_owner(step).start()
    own_at = pltpu.make_async_copy(a_send.at[gz], a_recv.at[gz], own_sem.at[3])
    own_at.start()

    def to_waves(step, part):
        peer = lax.rem(gy // 2 + step // 2, 8) * 2 + lax.rem(gy + step, 2)
        return pltpu.make_async_remote_copy(
            src_ref=send2[part].at[peer],
            dst_ref=recv2[part].at[gy],
            send_sem=sems2[part][0].at[step],
            recv_sem=sems2[part][1].at[step],
            device_id=(peer, gz),
            device_id_type=MESH,
        )

    def own_waves(part):
        return pltpu.make_async_copy(send2[part].at[gy], recv2[part].at[gy], own_sem.at[4 + part])

    def make_pair(turn, part):
        pair = lax.rem(gy // 2 + turn, 8)
        cols = pl.ds(pl.multiple_of(pair * 256, 256), 256)
        out = jnp.dot(recv1[part][...], first[:, cols], preferred_element_type=F32)
        for half in range(2):
            lanes = slice(half * 128, (half + 1) * 128)
            main = out[0 : MAIN[part], lanes]
            last = out[PIECE[part] : PIECE[part] + LAST[part], lanes]
            send2[part][pair * 2 + half] = pack(main, last, part).astype(BF16)

    def z_transform(part):
        own_plane(part).wait()

        @pl.loop(0, DEV - 1)
        def _(step):
            to_plane(step, part).wait()

        @pl.loop(0, DEV)
        def _(source):
            cols = pl.ds(pl.multiple_of(source * 128, 128), 128)
            piece = recv1[part][0 : PIECE[part], cols].astype(F32)
            recv1[part][PIECE[part] : WIDE[part], cols] = unpack_last(piece, part).astype(BF16)

        @pl.loop(1, 8)
        def _(turn):
            make_pair(turn, part)
            to_waves(2 * turn, part).start()
            to_waves(2 * turn + 1, part).start()

        make_pair(0, part)
        to_waves(1, part).start()
        own_waves(part).start()

    loads[2].wait()
    z_transform(0)
    z_transform(1)

    def y_lines(part):
        own_waves(part).wait()

        @pl.loop(1, DEV)
        def _(step):
            to_waves(step, part).wait()

        rows = SPLIT[part][1]
        depth = DEPTH[part] // 2
        quarter = depth // 4
        for comp in range(3):
            re_at, im_at = comp * KZL, (3 + comp) * KZL
            for third in range(3):
                at = (comp * 3 + third) * rows
                stacked = recv2[part][...].astype(F32)[:, at : at + rows].reshape(DEV * rows, 128)
                for piece in range(DEV * rows // 128):
                    tile = stacked[piece * 128 : (piece + 1) * 128].T
                    lo = third * quarter + piece * 128
                    cols, more = slice(lo, lo + 128), slice(depth + lo, depth + lo + 128)
                    real, imag = tile[0:KZL].astype(BF16), tile[KZL : 2 * KZL].astype(BF16)
                    left[part][re_at : re_at + KZL, cols] = real
                    left[part][re_at : re_at + KZL, more] = imag
                    left[part][im_at : im_at + KZL, cols] = imag
                    left[part][im_at : im_at + KZL, more] = -real
                    lo = 3 * quarter + piece * 128
                    cols, more = slice(lo, lo + 128), slice(depth + lo, depth + lo + 128)
                    for half in range(2):
                        value = tile[96 + half * 16 : 112 + half * 16].astype(BF16)
                        kz = third * 32 + half * 16
                        if kz < KZL:
                            left[part][re_at + kz : re_at + kz + 16, cols] = value
                            left[part][im_at + kz : im_at + kz + 16, more] = -value
                        else:
                            kz -= KZL
                            left[part][re_at + kz : re_at + kz + 16, more] = value
                            left[part][im_at + kz : im_at + kz + 16, cols] = value

    loads[3].wait()
    y_lines(0)

    @pl.loop(0, NY // 256)
    def _(tile):
        cols = pl.ds(pl.multiple_of(tile * 256, 256), 256)
        spec[:, cols] = jnp.dot(left_a[...], second[0 : DEPTH[0], cols], preferred_element_type=F32)

    own_at.wait()
    for step in range(1, DEV):
        to_owner(step).wait()
    at_ref[...] = a_recv[:, 0, :]

    y_lines(1)

    def write(tile):
        cols = pl.ds(pl.multiple_of(tile * 256, 256), 256)
        return pltpu.make_async_copy(spec.at[:, cols], spec_hbm.at[:, cols], out_sem.at[tile])

    @pl.loop(0, NY // 256)
    def _(tile):
        cols = pl.ds(pl.multiple_of(tile * 256, 256), 256)
        spec[:, cols] += jnp.dot(left_b[...], second[DEPTH[0] :, cols], preferred_element_type=F32)
        write(tile).start()

    @pl.loop(0, NY // 256)
    def _(tile):
        write(tile).wait()


def update_kernel(shift_ref, spec_ref, q_ref, u_ref, at_ref, count_ref, tvel_ref, q_out, u_out, t_out):
    rows = q_ref.shape[2]
    kz_first = lax.axis_index("gy") * KZL + pl.program_id(0) * rows
    shift = shift_ref[0]
    tiles_on, lanes_on = shift // 128, lax.rem(shift, 128)
    scale = 1.0 / math.sqrt(NY * NZ)
    kz = (lax.broadcasted_iota(jnp.int32, (rows, 128), 0) + kz_first).astype(F32)
    lane = lane_index((rows, 128))
    early = lane < lanes_on

    def turned(part, comp, tile):
        at = lax.rem(tile + 24 - tiles_on, 12)
        before = lax.rem(at + 11, 12)
        pieces = [
            spec_ref[part, comp, :, pl.ds(pl.multiple_of(place * 128, 128), 128)] for place in (before, at)
        ]
        return pltpu.roll(jnp.where(lane >= 128 - lanes_on, pieces[0], pieces[1]), lanes_on, 1)

    for tile in range(NY // 128):
        cols = slice(tile * 128, (tile + 1) * 128)
        kys = (lane + (tile * 128 if tile < 6 else tile * 128 - NY)).astype(F32)
        wave_square = kz * kz + kys * kys
        inverse = 1.0 / jnp.maximum(wave_square, 1.0)
        damping = (time_step * scale) * jnp.exp(-2.0 * wave_square / (NY * NZ))
        for part in range(2):
            moved = [turned(part, comp, tile) for comp in range(3)]
            radial = (kys * moved[1] + kz * moved[2]) * inverse
            projected = [moved[0], moved[1] - kys * radial, moved[2] - kz * radial]
            for comp in range(3):
                q_new = coef_keep * q_ref[part, comp, :, cols] + damping * projected[comp]
                q_out[part, comp, :, cols] = q_new
                u_out[part, comp, :, cols] = u_ref[part, comp, :, cols] + coef_add * q_new

    @pl.when(pl.program_id(0) == 0)
    def _():
        counts = jnp.broadcast_to(count_ref[...], (DEV, DEV))
        diagonal = lax.broadcasted_iota(jnp.int32, (DEV, DEV), 0) == lax.broadcasted_iota(jnp.int32, (DEV, DEV), 1)
        count_col = jnp.sum(jnp.where(diagonal, counts, 0).astype(F32), axis=1, keepdims=True)
        alive = (lane_index((DEV, TPP)).astype(F32) < count_col).astype(F32)
        for comp in range(3):
            old = tvel_ref[comp]
            at = at_ref[:, comp * TPP : (comp + 1) * TPP]
            t_out[comp] = old + relax_ratio * alive * (at - old)


def on_device(
    velocity,
    vorticity,
    q_state,
    u_state,
    shift,
    requests,
    tracer_slot,
    tracer_row,
    tracer_col,
    tracer_count,
    tracer_frac,
    tracer_vel,
):
    first, second = tables()
    hbm = pl.BlockSpec(memory_space=pl.ANY)
    vmem = pl.BlockSpec(memory_space=pltpu.VMEM)
    count = tracer_count.reshape(1, DEV)
    old = tracer_vel.reshape(3, DEV, TPP)
    spectrum, at_tracer = pl.pallas_call(
        exchange_kernel,
        out_shape=(
            jax.ShapeDtypeStruct((6 * KZL, NY), F32),
            jax.ShapeDtypeStruct((DEV, 128), F32),
        ),
        in_specs=[hbm] * 4 + [vmem] * 7,
        out_specs=(hbm, vmem),
        scratch_shapes=[
            pltpu.VMEM((3, CELL_ROWS, LOC), F32),
            pltpu.VMEM((3, CELL_ROWS, LOC), F32),
            pltpu.VMEM((PLANES, 3 * LOC, 128), F32),
            pltpu.VMEM((DEV * 128, DEV * 128), BF16),
            pltpu.VMEM((2 * NY, NY), BF16),
            pltpu.VMEM((256, 3072), BF16),
            pltpu.VMEM((TR, 256), BF16),
            pltpu.VMEM((TR, 3072), F32),
            pltpu.VMEM((2 * TR, 768), BF16),
            pltpu.VMEM((8, TR), F32),
            pltpu.VMEM((DEV, 2, 128), F32),
            pltpu.VMEM((DEV, 2, 128), F32),
            pltpu.VMEM((DEV, 1, 128), F32),
            pltpu.VMEM((DEV, 1, 128), F32),
            pltpu.VMEM((DEV, PIECE[0], 128), BF16),
            pltpu.VMEM((DEV, PIECE[1], 128), BF16),
            pltpu.VMEM((WIDE[0], DEV * 128), BF16),
            pltpu.VMEM((WIDE[1], DEV * 128), BF16),
            pltpu.VMEM((DEV, PIECE[0], 128), BF16),
            pltpu.VMEM((DEV, PIECE[1], 128), BF16),
            pltpu.VMEM((DEV, PIECE[0], 128), BF16),
            pltpu.VMEM((DEV, PIECE[1], 128), BF16),
            pltpu.VMEM((6 * KZL, DEPTH[0]), BF16),
            pltpu.VMEM((6 * KZL, DEPTH[1]), BF16),
            pltpu.VMEM((6 * KZL, NY), F32),
            pltpu.SemaphoreType.DMA((4,)),
            pltpu.SemaphoreType.DMA((6,)),
            pltpu.SemaphoreType.DMA((NY // 256,)),
        ]
        + [pltpu.SemaphoreType.DMA((DEV,))] * 12,
        compiler_params=pltpu.CompilerParams(
            collective_id=0, has_side_effects=True, vmem_limit_bytes=56 * 2**20
        ),
        cost_estimate=pl.CostEstimate(flops=6 * 10**9, bytes_accessed=25 * 2**20, transcendentals=0),
        name="exchange",
    )(
        velocity.reshape(3, CELL_ROWS, LOC),
        vorticity.reshape(3, CELL_ROWS, LOC),
        jnp.asarray(first),
        jnp.asarray(second),
        requests.reshape(DEV, 4),
        tracer_slot.reshape(DEV, TPP),
        tracer_row.reshape(DEV, TPP),
        tracer_col.reshape(DEV, TPP),
        count,
        tracer_frac.reshape(2, DEV, TPP),
        old,
    )
    rows = 8
    part = pl.BlockSpec((2, 3, rows, NY), lambda i: (0, 0, i, 0))

    def whole(*shape):
        return pl.BlockSpec(shape, lambda i: (0,) * len(shape))

    q_next, u_next, tracer_next = pl.pallas_call(
        update_kernel,
        grid=(KZL // rows,),
        out_shape=(
            jax.ShapeDtypeStruct((2, 3, KZL, NY), F32),
            jax.ShapeDtypeStruct((2, 3, KZL, NY), F32),
            jax.ShapeDtypeStruct((3, DEV, TPP), F32),
        ),
        in_specs=[
            pl.BlockSpec(memory_space=pltpu.SMEM),
            part,
            part,
            part,
            whole(DEV, 128),
            whole(1, DEV),
            whole(3, DEV, TPP),
        ],
        out_specs=(part, part, whole(3, DEV, TPP)),
        compiler_params=pltpu.CompilerParams(vmem_limit_bytes=60 * 2**20),
        name="update",
    )(
        shift,
        spectrum.reshape(2, 3, KZL, NY),
        q_state.reshape(2, 3, KZL, NY),
        u_state.reshape(2, 3, KZL, NY),
        at_tracer,
        count,
        old,
    )
    return (
        q_next.reshape(q_state.shape),
        u_next.reshape(u_state.shape),
        tracer_next.reshape(tracer_vel.shape),
    )


def solution(mesh):
    return jax.shard_map(
        on_device,
        mesh=mesh,
        in_specs=(
            P(None, None, "gy", "gz"),
            P(None, None, "gy", "gz"),
            P(None, None, "gz", "gy", None),
            P(None, None, "gz", "gy", None),
            P("gz"),
            P("gy", "gz", None, None),
            P("gy", "gz", None, None),
            P("gy", "gz", None, None),
            P("gy", "gz", None, None),
            P("gy", "gz", None),
            P(None, "gy", "gz", None, None),
            P(None, "gy", "gz", None, None),
        ),
        out_specs=(
            P(None, None, "gz", "gy", None),
            P(None, None, "gz", "gy", None),
            P(None, "gy", "gz", None, None),
        ),
        check_vma=False,
    )
```

time: 81.3 us -> 73.5 us (0.904)
  Pallas kernels: 76 us -> 70 us
  local copies, waits for them, and re-layouts: 3.68 us -> 1.36 us
    pallas_call x1, Pallas kernels: 72.4 us -> 63.6 us  [on_device(): pl.pallas_call(exchange_kernel, out_shape=(jax.ShapeDtypeStruct((6 * KZL,...]
    pallas_call x1, Pallas kernels: 3.68 us -> 6.35 us  [on_device(): pl.pallas_call(update_kernel, grid=(KZL // rows,), out_shape=(jax.ShapeDt...]
    unnamed x12 -> x0, local copies, waits for them, and re-layouts: 2.32 us -> none
where the time goes in v1:
time: 73.5 us; the launch traced here: 72.6 us
  Pallas kernels  70 us (95%)
  local copies, waits for them, and re-layouts  1.36 us (2%)
  between operations  1.29 us (2%)
    pallas_call x1, Pallas kernels, on_device(): pl.pallas_call(exchange_kernel, out_shape=(jax.ShapeDtypeStruct((6 * KZL,...  63.6 us
    pallas_call x1, Pallas kernels, on_device(): pl.pallas_call(update_kernel, grid=(KZL // rows,), out_shape=(jax.ShapeDt...  6.35 us

profile of v1, /device:TPU:1, one launch (start us, length us, event | category | flops | bytes accessed | tf_op | source)
XLA Modules:
  0.0 72.6 jit_solution(18159626577617546405)
XLA Ops:
  1.3 1.4 %copy.17.requests_ref = s32[16,4]{1,0:T(8,128)} copy(s32[16,4]{0,1:T(4,128)} %bitcast.34) | data formatting | bytes 512 | tf_op jit(solution)/shard_map/reshape | solution.py:623
  2.6 63.6 %exchange.1 = (f32[288,1536]{1,0:T(8,128)}, f32[16,128]{1,0:T(8,128)}) custom-call(f32[3,1536,96]{2,1,0:T(8,128)} %bitcast.21, f32[3,1536,96]{2,1,0:T(8,128)} %bitcast.22, bf16[2048,2048]{1,0:T(8,128)(2,1)} %constant.4.clone.first_hbm, bf16[3072,1536]{1,0:T(8,128)(2,1)} %constant.5.clone.second_hbm, s32[16,4]{1,0:T(8,128)} %copy.17.requests_ref, ...), custom_call_target="tpu_custom_call" | custom-call | flops 6000000000 | bytes 26214400 | tf_op jit(solution)/shard_map/exchange/pallas_call | solution.py:574
  66.3 6.4 %update.1 = (f32[2,3,48,1536]{3,2,1,0:T(8,128)}, f32[2,3,48,1536]{3,2,1,0:T(8,128)}, f32[3,16,32]{2,1,0:T(8,128)}) custom-call(s32[1]{0:T(128)S(6)} %copy.21.shift_ref, f32[2,3,48,1536]{3,2,1,0:T(8,128)} %bitcast.25, f32[2,3,48,1536]{3,2,1,0:T(8,128)} %bitcast.23, f32[2,3,48,1536]{3,2,1,0:T(8,128)} %bitcast.24, f32[16,128]{1,0:T(8,128)} %get-tuple-element.9.at_ref, ...), custom_call_target="tpu_custom_call" | custom-call | tf_op jit(solution)/shard_map/update/pallas_call | solution.py:637

commit v2 on v1

--- a/solution.py
+++ b/solution.py
@@ -30,6 +30,7 @@
 PIECE = (144, 80)
 LAST = (48, 24)
 WIDE = (192, 112)
+ROWS = 8
 DEPTH = (2048, 1024)
 
 drag_mass = 24.0
@@ -61,6 +62,13 @@
         row_of = (source * LOC + quarter * QUARTER + low + row).reshape(-1)
         second += [cos[row_of], sin[row_of]]
     return first.reshape(DEV * 128, DEV * 128), np.concatenate(second, axis=0)
+
+
+def choose(number, values):
+    out = values[-1]
+    for place in range(len(values) - 2, -1, -1):
+        out = jnp.where(number == place, values[place], out)
+    return out
 
 
 def lane_index(shape):
@@ -106,11 +114,26 @@
     return jnp.concatenate([block, jnp.zeros((block.shape[0], 128 - block.shape[1]), block.dtype)], axis=1)
 
 
+def as_column(row):
+    spread = jnp.broadcast_to(row, (DEV, DEV)).astype(F32)
+    diagonal = lax.broadcasted_iota(jnp.int32, (DEV, DEV), 0) == lax.broadcasted_iota(jnp.int32, (DEV, DEV), 1)
+    return jnp.sum(jnp.where(diagonal, spread, 0.0), axis=1, keepdims=True)
+
+
 def exchange_kernel(
     vel_hbm,
     vort_hbm,
     first_hbm,
     second_hbm,
+    requests_hbm,
+    slot_hbm,
+    row_hbm,
+    col_hbm,
+    count_hbm,
+    frac_hbm,
+    tvel_hbm,
+    spec_hbm,
+    at_ref,
     requests_ref,
     slot_ref,
     row_ref,
@@ -118,8 +141,6 @@
     count_ref,
     frac_ref,
     tvel_ref,
-    spec_hbm,
-    at_ref,
     vel,
     vort,
     cross,
@@ -146,6 +167,7 @@
     left_b,
     spec,
     load_sem,
+    small_sem,
     own_sem,
     out_sem,
     t_ssem,
@@ -184,19 +206,31 @@
         pltpu.make_async_copy(first_hbm, first, load_sem.at[2]),
         pltpu.make_async_copy(second_hbm, second, load_sem.at[3]),
     ]
-    for load in loads:
+    small = [
+        pltpu.make_async_copy(source, target, small_sem.at[number])
+        for number, (source, target) in enumerate(
+            (
+                (requests_hbm, requests_ref),
+                (slot_hbm, slot_ref),
+                (row_hbm, row_ref),
+                (col_hbm, col_ref),
+                (count_hbm, count_ref),
+                (frac_hbm, frac_ref),
+                (tvel_hbm, tvel_ref),
+            )
+        )
+    ]
+    for load in small + loads[0:2]:
         load.start()
+    for load in small:
+        load.wait()
 
     slots = slot_ref[...]
-    wanted = requests_ref[...]
-    block = jnp.zeros((DEV, TPP), jnp.int32)
+    block = jnp.zeros((DEV, TPP), F32)
     for number in range(4):
-        block = jnp.where(slots == number, wanted[:, number : number + 1], block)
-    counts = jnp.broadcast_to(count_ref[...], (DEV, DEV))
-    diagonal = lax.broadcasted_iota(jnp.int32, (DEV, DEV), 0) == lax.broadcasted_iota(jnp.int32, (DEV, DEV), 1)
-    count_col = jnp.sum(jnp.where(diagonal, counts, 0).astype(F32), axis=1, keepdims=True)
-    alive = (lane_index((DEV, TPP)).astype(F32) < count_col).astype(F32)
-    upper = [(block * 8 + row_ref[...]).astype(F32), col_ref[...].astype(F32), frac_ref[0], frac_ref[1]]
+        block = jnp.where(slots == number, as_column(requests_ref[number : number + 1, :]), block)
+    alive = (lane_index((DEV, TPP)).astype(F32) < as_column(count_ref[...])).astype(F32)
+    upper = [block * 8.0 + row_ref[...].astype(F32), col_ref[...].astype(F32), frac_ref[0], frac_ref[1]]
     lower = [tvel_ref[0], tvel_ref[1], tvel_ref[2], alive]
     t_send[:, 0, :] = jnp.concatenate(upper, axis=1)
     t_send[:, 1, :] = jnp.concatenate(lower, axis=1)
@@ -226,6 +260,8 @@
             vel_b[0:BLOCKS, cols] = widen(vel[comp, pl.ds(row, BLOCKS, stride=8), :]).astype(BF16)
     vel_b[BLOCKS:256, :] = jnp.zeros((256 - BLOCKS, 3072), BF16)
     loads[1].wait()
+    for load in loads[2:]:
+        load.start()
 
     @pl.loop(0, PLANES)
     def _(plane):
@@ -361,11 +397,6 @@
             to_plane(2 * turn + 1, 0).start()
 
     own_plane(0).start()
-
-    @pl.loop(0, DEV - 1)
-    def _(step):
-        to_plane(step, 1).start()
-
     own_plane(1).start()
 
     done = jnp.concatenate([back, jnp.zeros((128 - TPP, 128), F32)], axis=0).T
@@ -389,8 +420,21 @@
     own_at = pltpu.make_async_copy(a_send.at[gz], a_recv.at[gz], own_sem.at[3])
     own_at.start()
 
+    @pl.loop(0, DEV - 1)
+    def _(step):
+        to_plane(step, 0).wait_send()
+
+    @pl.loop(0, DEV - 1)
+    def _(step):
+        to_plane(step, 1).start()
+
+    def chip_of(turn):
+        dy = choose(turn, (1, 3, 2, 0, 2, 1, 3, 0))
+        dl = choose(turn, (1, 1, 1, 1, 0, 0, 0, 0))
+        return lax.rem(gy // 4 + dy, 4) * 2 + lax.rem(gy // 2 + dl, 2)
+
     def to_waves(step, part):
-        peer = lax.rem(gy // 2 + step // 2, 8) * 2 + lax.rem(gy + step, 2)
+        peer = chip_of(step // 2) * 2 + lax.rem(gy + step, 2)
         return pltpu.make_async_remote_copy(
             src_ref=send2[part].at[peer],
             dst_ref=recv2[part].at[gy],
@@ -404,7 +448,7 @@
         return pltpu.make_async_copy(send2[part].at[gy], recv2[part].at[gy], own_sem.at[4 + part])
 
     def make_pair(turn, part):
-        pair = lax.rem(gy // 2 + turn, 8)
+        pair = chip_of(turn)
         cols = pl.ds(pl.multiple_of(pair * 256, 256), 256)
         out = jnp.dot(recv1[part][...], first[:, cols], preferred_element_type=F32)
         for half in range(2):
@@ -418,7 +462,9 @@
 
         @pl.loop(0, DEV - 1)
         def _(step):
-            to_plane(step, part).wait()
+            if part == 1:
+                to_plane(step, part).wait_send()
+            to_plane(step, part).wait_recv()
 
         @pl.loop(0, DEV)
         def _(source):
@@ -426,14 +472,14 @@
             piece = recv1[part][0 : PIECE[part], cols].astype(F32)
             recv1[part][PIECE[part] : WIDE[part], cols] = unpack_last(piece, part).astype(BF16)
 
-        @pl.loop(1, 8)
+        @pl.loop(0, 7)
         def _(turn):
             make_pair(turn, part)
             to_waves(2 * turn, part).start()
             to_waves(2 * turn + 1, part).start()
 
-        make_pair(0, part)
-        to_waves(1, part).start()
+        make_pair(7, part)
+        to_waves(15, part).start()
         own_waves(part).start()
 
     loads[2].wait()
@@ -443,9 +489,11 @@
     def y_lines(part):
         own_waves(part).wait()
 
-        @pl.loop(1, DEV)
+        @pl.loop(0, DEV - 2)
         def _(step):
             to_waves(step, part).wait()
+
+        to_waves(15, part).wait()
 
         rows = SPLIT[part][1]
         depth = DEPTH[part] // 2
@@ -507,49 +555,87 @@
         write(tile).wait()
 
 
-def update_kernel(shift_ref, spec_ref, q_ref, u_ref, at_ref, count_ref, tvel_ref, q_out, u_out, t_out):
-    rows = q_ref.shape[2]
-    kz_first = lax.axis_index("gy") * KZL + pl.program_id(0) * rows
+def update_kernel(
+    shift_ref,
+    spec_hbm,
+    q_hbm,
+    u_hbm,
+    at_ref,
+    count_ref,
+    tvel_ref,
+    q_out,
+    u_out,
+    t_out,
+    spec,
+    q_state,
+    u_state,
+    in_sem,
+    out_sem,
+):
+    kz_first = lax.axis_index("gy") * KZL
     shift = shift_ref[0]
     tiles_on, lanes_on = shift // 128, lax.rem(shift, 128)
     scale = 1.0 / math.sqrt(NY * NZ)
-    kz = (lax.broadcasted_iota(jnp.int32, (rows, 128), 0) + kz_first).astype(F32)
-    lane = lane_index((rows, 128))
-    early = lane < lanes_on
-
-    def turned(part, comp, tile):
-        at = lax.rem(tile + 24 - tiles_on, 12)
-        before = lax.rem(at + 11, 12)
-        pieces = [
-            spec_ref[part, comp, :, pl.ds(pl.multiple_of(place * 128, 128), 128)] for place in (before, at)
-        ]
-        return pltpu.roll(jnp.where(lane >= 128 - lanes_on, pieces[0], pieces[1]), lanes_on, 1)
-
-    for tile in range(NY // 128):
-        cols = slice(tile * 128, (tile + 1) * 128)
-        kys = (lane + (tile * 128 if tile < 6 else tile * 128 - NY)).astype(F32)
-        wave_square = kz * kz + kys * kys
-        inverse = 1.0 / jnp.maximum(wave_square, 1.0)
-        damping = (time_step * scale) * jnp.exp(-2.0 * wave_square / (NY * NZ))
-        for part in range(2):
-            moved = [turned(part, comp, tile) for comp in range(3)]
-            radial = (kys * moved[1] + kz * moved[2]) * inverse
-            projected = [moved[0], moved[1] - kys * radial, moved[2] - kz * radial]
-            for comp in range(3):
-                q_new = coef_keep * q_ref[part, comp, :, cols] + damping * projected[comp]
-                q_out[part, comp, :, cols] = q_new
-                u_out[part, comp, :, cols] = u_ref[part, comp, :, cols] + coef_add * q_new
-
-    @pl.when(pl.program_id(0) == 0)
-    def _():
-        counts = jnp.broadcast_to(count_ref[...], (DEV, DEV))
-        diagonal = lax.broadcasted_iota(jnp.int32, (DEV, DEV), 0) == lax.broadcasted_iota(jnp.int32, (DEV, DEV), 1)
-        count_col = jnp.sum(jnp.where(diagonal, counts, 0).astype(F32), axis=1, keepdims=True)
-        alive = (lane_index((DEV, TPP)).astype(F32) < count_col).astype(F32)
-        for comp in range(3):
-            old = tvel_ref[comp]
-            at = at_ref[:, comp * TPP : (comp + 1) * TPP]
-            t_out[comp] = old + relax_ratio * alive * (at - old)
+    lane = lane_index((ROWS, 128))
+
+    def rows_of(ref, chunk):
+        return ref.at[:, :, pl.ds(pl.multiple_of(chunk * ROWS, ROWS), ROWS), :]
+
+    def arrive(number, chunk):
+        source, target = ((spec_hbm, spec), (q_hbm, q_state), (u_hbm, u_state))[number]
+        return pltpu.make_async_copy(rows_of(source, chunk), rows_of(target, chunk), in_sem.at[number, chunk])
+
+    def leave(number, chunk):
+        source, target = ((q_state, q_out), (u_state, u_out))[number]
+        return pltpu.make_async_copy(rows_of(source, chunk), rows_of(target, chunk), out_sem.at[number, chunk])
+
+    @pl.loop(0, KZL // ROWS)
+    def _(chunk):
+        for number in range(3):
+            arrive(number, chunk).start()
+
+    alive = (lane_index((DEV, TPP)).astype(F32) < as_column(count_ref[...])).astype(F32)
+    for comp in range(3):
+        old = tvel_ref[comp]
+        at = at_ref[:, comp * TPP : (comp + 1) * TPP]
+        t_out[comp] = old + relax_ratio * alive * (at - old)
+
+    @pl.loop(0, KZL // ROWS)
+    def _(chunk):
+        for number in range(3):
+            arrive(number, chunk).wait()
+        rows = pl.ds(pl.multiple_of(chunk * ROWS, ROWS), ROWS)
+        kz = (lax.broadcasted_iota(jnp.int32, (ROWS, 128), 0) + (kz_first + chunk * ROWS)).astype(F32)
+
+        def turned(part, comp, tile):
+            at = lax.rem(tile + 24 - tiles_on, 12)
+            before = lax.rem(at + 11, 12)
+            pieces = [
+                spec[part, comp, rows, pl.ds(pl.multiple_of(place * 128, 128), 128)] for place in (before, at)
+            ]
+            return pltpu.roll(jnp.where(lane >= 128 - lanes_on, pieces[0], pieces[1]), lanes_on, 1)
+
+        for tile in range(NY // 128):
+            cols = slice(tile * 128, (tile + 1) * 128)
+            kys = (lane + (tile * 128 if tile < 6 else tile * 128 - NY)).astype(F32)
+            wave_square = kz * kz + kys * kys
+            inverse = 1.0 / jnp.maximum(wave_square, 1.0)
+            damping = (time_step * scale) * jnp.exp(-2.0 * wave_square / (NY * NZ))
+            for part in range(2):
+                moved = [turned(part, comp, tile) for comp in range(3)]
+                radial = (kys * moved[1] + kz * moved[2]) * inverse
+                projected = [moved[0], moved[1] - kys * radial, moved[2] - kz * radial]
+                for comp in range(3):
+                    q_new = coef_keep * q_state[part, comp, rows, cols] + damping * projected[comp]
+                    q_state[part, comp, rows, cols] = q_new
+                    u_state[part, comp, rows, cols] += coef_add * q_new
+        for number in range(2):
+            leave(number, chunk).start()
+
+    @pl.loop(0, KZL // ROWS)
+    def _(chunk):
+        for number in range(2):
+            leave(number, chunk).wait()
 
 
 def on_device(
@@ -577,9 +663,16 @@
             jax.ShapeDtypeStruct((6 * KZL, NY), F32),
             jax.ShapeDtypeStruct((DEV, 128), F32),
         ),
-        in_specs=[hbm] * 4 + [vmem] * 7,
+        in_specs=[hbm] * 11,
         out_specs=(hbm, vmem),
         scratch_shapes=[
+            pltpu.VMEM((4, DEV), jnp.int32),
+            pltpu.VMEM((DEV, TPP), jnp.int32),
+            pltpu.VMEM((DEV, TPP), jnp.int32),
+            pltpu.VMEM((DEV, TPP), jnp.int32),
+            pltpu.VMEM((1, DEV), jnp.int32),
+            pltpu.VMEM((2, DEV, TPP), F32),
+            pltpu.VMEM((3, DEV, TPP), F32),
             pltpu.VMEM((3, CELL_ROWS, LOC), F32),
             pltpu.VMEM((3, CELL_ROWS, LOC), F32),
             pltpu.VMEM((PLANES, 3 * LOC, 128), F32),
@@ -606,6 +699,7 @@
             pltpu.VMEM((6 * KZL, DEPTH[1]), BF16),
             pltpu.VMEM((6 * KZL, NY), F32),
             pltpu.SemaphoreType.DMA((4,)),
+            pltpu.SemaphoreType.DMA((7,)),
             pltpu.SemaphoreType.DMA((6,)),
             pltpu.SemaphoreType.DMA((NY // 256,)),
         ]
@@ -620,7 +714,7 @@
         vorticity.reshape(3, CELL_ROWS, LOC),
         jnp.asarray(first),
         jnp.asarray(second),
-        requests.reshape(DEV, 4),
+        requests.reshape(DEV, 4).T,
         tracer_slot.reshape(DEV, TPP),
         tracer_row.reshape(DEV, TPP),
         tracer_col.reshape(DEV, TPP),
@@ -628,15 +722,8 @@
         tracer_frac.reshape(2, DEV, TPP),
         old,
     )
-    rows = 8
-    part = pl.BlockSpec((2, 3, rows, NY), lambda i: (0, 0, i, 0))
-
-    def whole(*shape):
-        return pl.BlockSpec(shape, lambda i: (0,) * len(shape))
-
     q_next, u_next, tracer_next = pl.pallas_call(
         update_kernel,
-        grid=(KZL // rows,),
         out_shape=(
             jax.ShapeDtypeStruct((2, 3, KZL, NY), F32),
             jax.ShapeDtypeStruct((2, 3, KZL, NY), F32),
@@ -644,14 +731,21 @@
         ),
         in_specs=[
             pl.BlockSpec(memory_space=pltpu.SMEM),
-            part,
-            part,
-            part,
-            whole(DEV, 128),
-            whole(1, DEV),
-            whole(3, DEV, TPP),
+            hbm,
+            hbm,
+            hbm,
+            vmem,
+            vmem,
+            vmem,
         ],
-        out_specs=(part, part, whole(3, DEV, TPP)),
+        out_specs=(hbm, hbm, vmem),
+        scratch_shapes=[
+            pltpu.VMEM((2, 3, KZL, NY), F32),
+            pltpu.VMEM((2, 3, KZL, NY), F32),
+            pltpu.VMEM((2, 3, KZL, NY), F32),
+            pltpu.SemaphoreType.DMA((3, KZL // ROWS)),
+            pltpu.SemaphoreType.DMA((2, KZL // ROWS)),
+        ],
         compiler_params=pltpu.CompilerParams(vmem_limit_bytes=60 * 2**20),
         name="update",
     )(

time: 73.5 us -> 66.9 us (0.910)
  Pallas kernels: 70 us -> 65.5 us
  local copies, waits for them, and re-layouts: 1.36 us -> 0 us
    pallas_call x1, Pallas kernels: 63.6 us -> 59.8 us  [on_device(): pl.pallas_call(exchange_kernel, out_shape=(jax.ShapeDtypeStruct((6 * KZL,...]
    reshape x1 -> x0, local copies, waits for them, and re-layouts: 1.36 us -> none  [on_device(): requests.reshape(DEV, 4)]
where the time goes in v2:
time: 66.9 us; the launch traced here: 66.8 us
  Pallas kernels  65.5 us (98%)
  between operations  1.29 us (2%)
    pallas_call x1, Pallas kernels, on_device(): pl.pallas_call(exchange_kernel, out_shape=(jax.ShapeDtypeStruct((6 * KZL,...  59.8 us
    pallas_call x1, Pallas kernels, on_device(): pl.pallas_call(update_kernel, out_shape=(jax.ShapeDtypeStruct((2, 3, KZL,...  5.7 us

profile of v2, /device:TPU:1, one launch (start us, length us, event | category | flops | bytes accessed | tf_op | source)
XLA Modules:
  0.0 66.8 jit_solution(2309998312397454960)
XLA Ops:
  1.3 59.8 %exchange.1 = (f32[288,1536]{1,0:T(8,128)}, f32[16,128]{1,0:T(8,128)}) custom-call(f32[3,1536,96]{2,1,0:T(8,128)} %bitcast.23, f32[3,1536,96]{2,1,0:T(8,128)} %bitcast.24, bf16[2048,2048]{1,0:T(8,128)(2,1)} %constant.4.clone.first_hbm, bf16[3072,1536]{1,0:T(8,128)(2,1)} %constant.5.clone.second_hbm, s32[4,16]{1,0:T(4,128)} %bitcast.36, s32[16,32]{1,0:T(8,128)} %bitcast.31, ...), custom_call_target="tpu_custom_call" | custom-call | flops 6000000000 | bytes 26214400 | tf_op jit(solution)/shard_map/exchange/pallas_call | solution.py:660
  61.0 5.7 %update.1 = (f32[2,3,48,1536]{3,2,1,0:T(8,128)}, f32[2,3,48,1536]{3,2,1,0:T(8,128)}, f32[3,16,32]{2,1,0:T(8,128)}) custom-call(s32[1]{0:T(128)S(6)} %copy.20.shift_ref, f32[2,3,48,1536]{3,2,1,0:T(8,128)} %bitcast.27, f32[2,3,48,1536]{3,2,1,0:T(8,128)} %bitcast.25, f32[2,3,48,1536]{3,2,1,0:T(8,128)} %bitcast.26, f32[16,128]{1,0:T(8,128)} %get-tuple-element.9.at_ref, ...), custom_call_target="tpu_custom_call" | custom-call | tf_op jit(solution)/shard_map/update/pallas_call | solution.py:725

commit v3 on v2

--- a/solution.py
+++ b/solution.py
@@ -30,7 +30,7 @@
 PIECE = (144, 80)
 LAST = (48, 24)
 WIDE = (192, 112)
-ROWS = 8
+ROWS = 16
 DEPTH = (2048, 1024)
 
 drag_mass = 24.0
@@ -133,7 +133,6 @@
     frac_hbm,
     tvel_hbm,
     spec_hbm,
-    at_ref,
     requests_ref,
     slot_ref,
     row_ref,
@@ -531,12 +530,13 @@
     @pl.loop(0, NY // 256)
     def _(tile):
         cols = pl.ds(pl.multiple_of(tile * 256, 256), 256)
-        spec[:, cols] = jnp.dot(left_a[...], second[0 : DEPTH[0], cols], preferred_element_type=F32)
+        spec[0 : 6 * KZL, cols] = jnp.dot(left_a[...], second[0 : DEPTH[0], cols], preferred_element_type=F32)
 
     own_at.wait()
     for step in range(1, DEV):
         to_owner(step).wait()
-    at_ref[...] = a_recv[:, 0, :]
+    spec[6 * KZL :, :] = jnp.zeros((DEV, NY), F32)
+    spec[6 * KZL :, 0:128] = a_recv[:, 0, :]
 
     y_lines(1)
 
@@ -547,7 +547,7 @@
     @pl.loop(0, NY // 256)
     def _(tile):
         cols = pl.ds(pl.multiple_of(tile * 256, 256), 256)
-        spec[:, cols] += jnp.dot(left_b[...], second[DEPTH[0] :, cols], preferred_element_type=F32)
+        spec[0 : 6 * KZL, cols] += jnp.dot(left_b[...], second[DEPTH[0] :, cols], preferred_element_type=F32)
         write(tile).start()
 
     @pl.loop(0, NY // 256)
@@ -557,19 +557,16 @@
 
 def update_kernel(
     shift_ref,
-    spec_hbm,
-    q_hbm,
-    u_hbm,
-    at_ref,
+    spec,
+    q_ref,
+    u_ref,
     count_ref,
     tvel_ref,
     q_out,
     u_out,
     t_out,
-    spec,
-    q_state,
-    u_state,
-    in_sem,
+    q_new_ref,
+    u_new_ref,
     out_sem,
 ):
     kz_first = lax.axis_index("gy") * KZL
@@ -581,38 +578,26 @@
     def rows_of(ref, chunk):
         return ref.at[:, :, pl.ds(pl.multiple_of(chunk * ROWS, ROWS), ROWS), :]
 
-    def arrive(number, chunk):
-        source, target = ((spec_hbm, spec), (q_hbm, q_state), (u_hbm, u_state))[number]
-        return pltpu.make_async_copy(rows_of(source, chunk), rows_of(target, chunk), in_sem.at[number, chunk])
-
     def leave(number, chunk):
-        source, target = ((q_state, q_out), (u_state, u_out))[number]
+        source, target = ((q_new_ref, q_out), (u_new_ref, u_out))[number]
         return pltpu.make_async_copy(rows_of(source, chunk), rows_of(target, chunk), out_sem.at[number, chunk])
-
-    @pl.loop(0, KZL // ROWS)
-    def _(chunk):
-        for number in range(3):
-            arrive(number, chunk).start()
 
     alive = (lane_index((DEV, TPP)).astype(F32) < as_column(count_ref[...])).astype(F32)
     for comp in range(3):
         old = tvel_ref[comp]
-        at = at_ref[:, comp * TPP : (comp + 1) * TPP]
+        at = spec[6 * KZL :, comp * TPP : (comp + 1) * TPP]
         t_out[comp] = old + relax_ratio * alive * (at - old)
 
     @pl.loop(0, KZL // ROWS)
     def _(chunk):
-        for number in range(3):
-            arrive(number, chunk).wait()
         rows = pl.ds(pl.multiple_of(chunk * ROWS, ROWS), ROWS)
         kz = (lax.broadcasted_iota(jnp.int32, (ROWS, 128), 0) + (kz_first + chunk * ROWS)).astype(F32)
 
         def turned(part, comp, tile):
             at = lax.rem(tile + 24 - tiles_on, 12)
             before = lax.rem(at + 11, 12)
-            pieces = [
-                spec[part, comp, rows, pl.ds(pl.multiple_of(place * 128, 128), 128)] for place in (before, at)
-            ]
+            lines = pl.ds(pl.multiple_of((part * 3 + comp) * KZL + chunk * ROWS, ROWS), ROWS)
+            pieces = [spec[lines, pl.ds(pl.multiple_of(place * 128, 128), 128)] for place in (before, at)]
             return pltpu.roll(jnp.where(lane >= 128 - lanes_on, pieces[0], pieces[1]), lanes_on, 1)
 
         for tile in range(NY // 128):
@@ -626,9 +611,9 @@
                 radial = (kys * moved[1] + kz * moved[2]) * inverse
                 projected = [moved[0], moved[1] - kys * radial, moved[2] - kz * radial]
                 for comp in range(3):
-                    q_new = coef_keep * q_state[part, comp, rows, cols] + damping * projected[comp]
-                    q_state[part, comp, rows, cols] = q_new
-                    u_state[part, comp, rows, cols] += coef_add * q_new
+                    q_new = coef_keep * q_ref[part, comp, rows, cols] + damping * projected[comp]
+                    q_new_ref[part, comp, rows, cols] = q_new
+                    u_new_ref[part, comp, rows, cols] = u_ref[part, comp, rows, cols] + coef_add * q_new
         for number in range(2):
             leave(number, chunk).start()
 
@@ -657,14 +642,11 @@
     vmem = pl.BlockSpec(memory_space=pltpu.VMEM)
     count = tracer_count.reshape(1, DEV)
     old = tracer_vel.reshape(3, DEV, TPP)
-    spectrum, at_tracer = pl.pallas_call(
+    spectrum = pl.pallas_call(
         exchange_kernel,
-        out_shape=(
-            jax.ShapeDtypeStruct((6 * KZL, NY), F32),
-            jax.ShapeDtypeStruct((DEV, 128), F32),
-        ),
+        out_shape=jax.ShapeDtypeStruct((6 * KZL + DEV, NY), F32),
         in_specs=[hbm] * 11,
-        out_specs=(hbm, vmem),
+        out_specs=hbm,
         scratch_shapes=[
             pltpu.VMEM((4, DEV), jnp.int32),
             pltpu.VMEM((DEV, TPP), jnp.int32),
@@ -697,7 +679,7 @@
             pltpu.VMEM((DEV, PIECE[1], 128), BF16),
             pltpu.VMEM((6 * KZL, DEPTH[0]), BF16),
             pltpu.VMEM((6 * KZL, DEPTH[1]), BF16),
-            pltpu.VMEM((6 * KZL, NY), F32),
+            pltpu.VMEM((6 * KZL + DEV, NY), F32),
             pltpu.SemaphoreType.DMA((4,)),
             pltpu.SemaphoreType.DMA((7,)),
             pltpu.SemaphoreType.DMA((6,)),
@@ -731,9 +713,8 @@
         ),
         in_specs=[
             pl.BlockSpec(memory_space=pltpu.SMEM),
-            hbm,
-            hbm,
-            hbm,
+            vmem,
+            vmem,
             vmem,
             vmem,
             vmem,
@@ -742,18 +723,15 @@
         scratch_shapes=[
             pltpu.VMEM((2, 3, KZL, NY), F32),
             pltpu.VMEM((2, 3, KZL, NY), F32),
-            pltpu.VMEM((2, 3, KZL, NY), F32),
-            pltpu.SemaphoreType.DMA((3, KZL // ROWS)),
             pltpu.SemaphoreType.DMA((2, KZL // ROWS)),
         ],
-        compiler_params=pltpu.CompilerParams(vmem_limit_bytes=60 * 2**20),
+        compiler_params=pltpu.CompilerParams(vmem_limit_bytes=32 * 2**20),
         name="update",
     )(
         shift,
-        spectrum.reshape(2, 3, KZL, NY),
+        spectrum,
         q_state.reshape(2, 3, KZL, NY),
         u_state.reshape(2, 3, KZL, NY),
-        at_tracer,
         count,
         old,
     )

time: 66.9 us -> 65 us (0.972)
  Pallas kernels: 65.5 us -> 62 us
  local copies, waits for them, and re-layouts: 0 us -> 1.52 us
    pallas_call x1, Pallas kernels: 5.7 us -> 2.9 us  [on_device(): pl.pallas_call(update_kernel, out_shape=(jax.ShapeDtypeStruct((2, 3, KZL,...]
    unnamed x0 -> x10, local copies, waits for them, and re-layouts: none -> 1.52 us
where the time goes in v3:
time: 65 us; the launch traced here: 64.9 us
  Pallas kernels  62 us (95%)
  local copies, waits for them, and re-layouts  1.52 us (2%)
  between operations  1.36 us (2%)
    pallas_call x1, Pallas kernels, on_device(): pl.pallas_call(exchange_kernel, out_shape=jax.ShapeDtypeStruct((6 * KZL +...  59.1 us
    pallas_call x1, Pallas kernels, on_device(): pl.pallas_call(update_kernel, out_shape=(jax.ShapeDtypeStruct((2, 3, KZL,...  2.9 us
    unnamed x10, local copies, waits for them, and re-layouts  1.52 us

profile of v3, /device:TPU:1, one launch (start us, length us, event | category | flops | bytes accessed | tf_op | source)
XLA Modules:
  0.0 64.9 jit_solution(10023390348930161849)
XLA Ops:
  1.3 0.0 copy-start.1
  1.3 0.0 copy-start.2
  1.3 0.0 copy-start.3
  1.3 0.0 copy-start.4
  1.3 59.1 %exchange.1.spec = f32[304,1536]{1,0:T(8,128)} custom-call(f32[3,1536,96]{2,1,0:T(8,128)} %bitcast.28, f32[3,1536,96]{2,1,0:T(8,128)} %bitcast.29, bf16[2048,2048]{1,0:T(8,128)(2,1)} %constant.4.clone.first_hbm, bf16[3072,1536]{1,0:T(8,128)(2,1)} %constant.5.clone.second_hbm, s32[4,16]{1,0:T(4,128)} %bitcast.34, s32[16,32]{1,0:T(8,128)} %bitcast.31, ...), custom_call_target="tpu_custom_call" | custom-call | flops 6000000000 | bytes 26214400 | tf_op jit(solution)/shard_map/exchange/pallas_call | solution.py:645
  60.5 0.0 copy-done.1
  60.5 0.0 copy-done.2
  60.5 0.0 copy-done.3
  60.5 0.0 copy-done.4
  60.5 0.0 copy-start
  60.5 1.5 %copy-done = f32[304,1536]{1,0:T(8,128)S(1)} copy-done((f32[304,1536]{1,0:T(8,128)S(1)}, f32[304,1536]{1,0:T(8,128)}, u32[]{:S(2)}) %copy-start) | copy-done | bytes 1867800
  62.0 2.9 %update.1 = (f32[2,3,48,1536]{3,2,1,0:T(8,128)}, f32[2,3,48,1536]{3,2,1,0:T(8,128)}, f32[3,16,32]{2,1,0:T(8,128)}) custom-call(s32[1]{0:T(128)S(6)} %copy.20.shift_ref, f32[304,1536]{1,0:T(8,128)S(1)} %copy-done, f32[2,3,48,1536]{3,2,1,0:T(8,128)S(1)} %bitcast.22, f32[2,3,48,1536]{3,2,1,0:T(8,128)S(1)} %bitcast.23, s32[1,16]{1,0:T(1,128)S(1)} %bitcast.27, ...), custom_call_target="tpu_custom_call" | custom-call | tf_op jit(solution)/shard_map/update/pallas_call | solution.py:707
Async XLA Ops:
  1.3 59.2 %copy-start.1 = (f32[2,3,1,48,1536]{4,3,2,1,0:T(8,128)S(1)}, f32[2,3,1,48,1536]{4,3,2,1,0:T(8,128)}, u32[]{:S(2)}) copy-start(f32[2,3,1,48,1536]{4,3,2,1,0:T(8,128)} %param.16) | copy-start | bytes 5308420
  1.3 59.2 %copy-start.2 = (f32[2,3,1,48,1536]{4,3,2,1,0:T(8,128)S(1)}, f32[2,3,1,48,1536]{4,3,2,1,0:T(8,128)}, u32[]{:S(2)}) copy-start(f32[2,3,1,48,1536]{4,3,2,1,0:T(8,128)} %param.17) | copy-start | bytes 5308420
  1.3 59.2 %copy-start.3 = (f32[3,1,1,16,32]{4,3,2,1,0:T(8,128)S(1)}, f32[3,1,1,16,32]{4,3,2,1,0:T(8,128)}, u32[]{:S(2)}) copy-start(f32[3,1,1,16,32]{4,3,2,1,0:T(8,128)} %param.25) | copy-start | bytes 18436
  1.3 59.2 %copy-start.4 = (s32[1,1,16]{2,1,0:T(1,128)S(1)}, s32[1,1,16]{2,1,0:T(1,128)}, u32[]{:S(2)}) copy-start(s32[1,1,16]{2,1,0:T(1,128)} %param.23) | copy-start | bytes 196
  60.5 1.5 %copy-start = (f32[304,1536]{1,0:T(8,128)S(1)}, f32[304,1536]{1,0:T(8,128)}, u32[]{:S(2)}) copy-start(f32[304,1536]{1,0:T(8,128)} %exchange.1.spec) | copy-start | bytes 5603332

commit v4 on v3

--- a/solution.py
+++ b/solution.py
@@ -333,11 +333,9 @@
                 spread[place, comp * 256 : comp * 256 + 128] = high
                 spread[place, comp * 256 + 128 : (comp + 1) * 256] = (value - high.astype(F32)).astype(BF16)
 
-    def far(number):
-        return jnp.where(number == 0, 2, jnp.where(number == 1, 1, jnp.where(number == 2, 3, 0)))
-
     def plane_of(step):
-        dx, dh = far(lax.rem(step, 4)), far(step // 4)
+        dx = choose(step, (2, 1, 2, 2, 3, 0, 1, 1, 3, 3, 0, 0, 2, 1, 3, 0))
+        dh = choose(step, (2, 2, 1, 3, 2, 2, 1, 3, 1, 3, 1, 3, 0, 0, 0, 0))
         return lax.rem(my_x + dx, 4) * 4 + lax.rem(my_h + dh, 4)
 
     def landing(part):

time: 65 us -> 64.7 us (level)
  no operation moved by 1% of the time
where the time goes in v4:
time: 64.7 us; the launch traced here: 64.6 us
  Pallas kernels  61.8 us (96%)
  local copies, waits for them, and re-layouts  1.52 us (2%)
  between operations  1.36 us (2%)
    pallas_call x1, Pallas kernels, on_device(): pl.pallas_call(exchange_kernel, out_shape=jax.ShapeDtypeStruct((6 * KZL +...  58.9 us
    pallas_call x1, Pallas kernels, on_device(): pl.pallas_call(update_kernel, out_shape=(jax.ShapeDtypeStruct((2, 3, KZL,...  2.9 us
    unnamed x10, local copies, waits for them, and re-layouts  1.52 us

profile of v4, /device:TPU:1, one launch (start us, length us, event | category | flops | bytes accessed | tf_op | source)
XLA Modules:
  0.0 64.6 jit_solution(4485220509211202038)
XLA Ops:
  1.3 0.0 copy-start.1
  1.3 0.0 copy-start.2
  1.3 0.0 copy-start.3
  1.3 0.0 copy-start.4
  1.3 58.9 %exchange.1.spec = f32[304,1536]{1,0:T(8,128)} custom-call(f32[3,1536,96]{2,1,0:T(8,128)} %bitcast.28, f32[3,1536,96]{2,1,0:T(8,128)} %bitcast.29, bf16[2048,2048]{1,0:T(8,128)(2,1)} %constant.4.clone.first_hbm, bf16[3072,1536]{1,0:T(8,128)(2,1)} %constant.5.clone.second_hbm, s32[4,16]{1,0:T(4,128)} %bitcast.34, s32[16,32]{1,0:T(8,128)} %bitcast.31, ...), custom_call_target="tpu_custom_call" | custom-call | flops 6000000000 | bytes 26214400 | tf_op jit(solution)/shard_map/exchange/pallas_call | solution.py:643
  60.2 0.0 copy-done.1
  60.2 0.0 copy-done.2
  60.2 0.0 copy-done.3
  60.2 0.0 copy-done.4
  60.2 0.0 copy-start
  60.2 1.5 %copy-done = f32[304,1536]{1,0:T(8,128)S(1)} copy-done((f32[304,1536]{1,0:T(8,128)S(1)}, f32[304,1536]{1,0:T(8,128)}, u32[]{:S(2)}) %copy-start) | copy-done | bytes 1867800
  61.7 2.9 %update.1 = (f32[2,3,48,1536]{3,2,1,0:T(8,128)}, f32[2,3,48,1536]{3,2,1,0:T(8,128)}, f32[3,16,32]{2,1,0:T(8,128)}) custom-call(s32[1]{0:T(128)S(6)} %copy.20.shift_ref, f32[304,1536]{1,0:T(8,128)S(1)} %copy-done, f32[2,3,48,1536]{3,2,1,0:T(8,128)S(1)} %bitcast.22, f32[2,3,48,1536]{3,2,1,0:T(8,128)S(1)} %bitcast.23, s32[1,16]{1,0:T(1,128)S(1)} %bitcast.27, ...), custom_call_target="tpu_custom_call" | custom-call | tf_op jit(solution)/shard_map/update/pallas_call | solution.py:705
Async XLA Ops:
  1.3 58.9 %copy-start.1 = (f32[2,3,1,48,1536]{4,3,2,1,0:T(8,128)S(1)}, f32[2,3,1,48,1536]{4,3,2,1,0:T(8,128)}, u32[]{:S(2)}) copy-start(f32[2,3,1,48,1536]{4,3,2,1,0:T(8,128)} %param.16) | copy-start | bytes 5308420
  1.3 58.9 %copy-start.2 = (f32[2,3,1,48,1536]{4,3,2,1,0:T(8,128)S(1)}, f32[2,3,1,48,1536]{4,3,2,1,0:T(8,128)}, u32[]{:S(2)}) copy-start(f32[2,3,1,48,1536]{4,3,2,1,0:T(8,128)} %param.17) | copy-start | bytes 5308420
  1.3 58.9 %copy-start.3 = (f32[3,1,1,16,32]{4,3,2,1,0:T(8,128)S(1)}, f32[3,1,1,16,32]{4,3,2,1,0:T(8,128)}, u32[]{:S(2)}) copy-start(f32[3,1,1,16,32]{4,3,2,1,0:T(8,128)} %param.25) | copy-start | bytes 18436
  1.3 58.9 %copy-start.4 = (s32[1,1,16]{2,1,0:T(1,128)S(1)}, s32[1,1,16]{2,1,0:T(1,128)}, u32[]{:S(2)}) copy-start(s32[1,1,16]{2,1,0:T(1,128)} %param.23) | copy-start | bytes 196
  60.2 1.5 %copy-start = (f32[304,1536]{1,0:T(8,128)S(1)}, f32[304,1536]{1,0:T(8,128)}, u32[]{:S(2)}) copy-start(f32[304,1536]{1,0:T(8,128)} %exchange.1.spec) | copy-start | bytes 5603332
